TPU v7x, 32 devices: a whole 2x2x4 slice. The times are simulated.
32 devices in a mesh: rows: 8 (over z, y), blk: 4 (over x, core).
Axes of the slice: x: 2, y: 2, z: 4, core: 2. Of those that a mesh axis runs over, the one named last changes fastest.
Arguments:
- acol: int32 [128, 32], P('rows', 'blk'), may hold values from -1 to 127, as said below
- aval: bfloat16 [128, 32, 128, 128], P('rows', 'blk'), may hold values from -0.109375 to 0.109375
- mcol: int32 [2, 128, 4], P(None, 'rows'), may hold values from 0 to 63, as said below
- mval: bfloat16 [2, 128, 4, 128, 128], P(None, 'rows'), may hold values from -12 to 12
- rpat: int32 [2, 128, 2], P(None, 'rows'), may hold values from 0 to 63, as said below
- scol: int32 [2, 64], replicated, may hold values from 0 to 127, as said below
- cand: int32 [2, 128, 2], P(None, 'rows'), may hold values from 0 to 63, as said below
Outputs:
- resid: bfloat16 [2, 128, 2, 128, 128], P(None, 'rows', None, None, 'blk')
- scores: float32 [2, 128, 2, 128], P(None, 'rows', None, 'blk')
Inputs may be any that keep to these rules, and one draw needn't show every extreme that they name: `acol`: each block row lists 27 different block columns, each at most 16 block rows from the row itself, counted cyclically modulo 128; its other 5 entries are -1. `mcol`: the entries of one block row in one slab differ. `rpat`: the entries of one block row in one slab differ. `scol`: the entries of one slab differ. `cand`: the entries of one block row in one slab differ.
All inputs are finite; a program needn't handle non-finite values.
Results may differ from a plain program's by a relative error of at most 0.0025.
Values may be sent and summed in bfloat16 or wider, within the bound.
No kernel may reach another device: no remote copies, remote signals or barrier semaphores. Data moves between devices by JAX's collectives and lax.ppermute only.
A program may use at most 128 MiB of HBM per device.

v0:
```python
import functools

import jax
import jax.numpy as jnp
from jax import lax
from jax.experimental import pallas as pl
from jax.experimental.pallas import tpu as pltpu
from jax.sharding import PartitionSpec as P


def product_sums(
    n_blocks, t_counts, n_picks, finish, pick_ref, start_ref, extra_ref, *refs
):
    n_tables = len(t_counts)
    a_refs = refs[:n_blocks]
    t_refs = refs[n_blocks : n_blocks + n_tables]
    out_ref, a_tab, tab, a_sems, t_sems = refs[n_blocks + n_tables :]
    rows, slots, size = a_tab.shape[:3]
    per_piece = slots // n_blocks

    def table_copy(piece):
        return pltpu.make_async_copy(
            t_refs[piece], tab.at[pl.ds(start_ref[piece], t_counts[piece])], t_sems.at[piece]
        )

    def block_copy(row, piece):
        return pltpu.make_async_copy(
            a_refs[piece].at[row],
            a_tab.at[row, pl.ds(piece * per_piece, per_piece)],
            a_sems.at[row, piece],
        )

    for piece in range(n_blocks):
        block_copy(0, piece).start()
    for piece in range(n_tables):
        table_copy(piece).start()
    for row in range(1, rows):
        for piece in range(n_blocks):
            block_copy(row, piece).start()
    tab[tab.shape[0] - 1] = jnp.zeros(tab.shape[1:], tab.dtype)
    for piece in range(n_tables):
        table_copy(piece).wait()

    def one_row(row, carry):
        for piece in range(n_blocks):
            block_copy(row, piece).wait()
        total = jnp.zeros((size, n_picks * size), jnp.float32)
        for slot in range(0, slots, 2):
            left = jnp.concatenate([a_tab[row, slot], a_tab[row, slot + 1]], axis=1)
            at = (row * slots + slot) * n_picks
            right = jnp.concatenate(
                [
                    jnp.concatenate(
                        [tab[pick_ref[at + k * n_picks + p]] for p in range(n_picks)], axis=1
                    )
                    for k in range(2)
                ],
                axis=0,
            )
            total += jnp.dot(left, right, preferred_element_type=jnp.float32)
        finish(row, total, extra_ref, out_ref)
        return carry

    lax.fori_loop(0, rows, one_row, 0)


def cut_rows(counts, pieces, start_ref, *refs):
    n = len(counts)
    sources, outs = refs[:n], refs[n : 2 * n]
    stages, in_sems, out_sems = refs[2 * n : 3 * n], refs[3 * n], refs[3 * n + 1]

    def copy_in(k, p):
        size = counts[k] // pieces
        return pltpu.make_async_copy(
            sources[k].at[pl.ds(start_ref[k] + p * size, size)],
            stages[k].at[pl.ds(p * size, size)],
            in_sems.at[k, p],
        )

    def copy_out(k, p):
        part = pl.ds(p * (counts[k] // pieces), counts[k] // pieces)
        return pltpu.make_async_copy(stages[k].at[part], outs[k].at[part], out_sems.at[k, p])

    every = [(k, p) for k in range(n) for p in range(pieces)]
    for k, p in every:
        copy_in(k, p).start()
    for k, p in every:
        copy_in(k, p).wait()
        copy_out(k, p).start()
    for k, p in every:
        copy_out(k, p).wait()


def in_hbm(array):
    return pltpu.with_memory_space_constraint(array, pltpu.HBM)


def call_cut(*jobs):
    counts = [count for _, _, count in jobs]
    pieces = 4
    anywhere = pl.BlockSpec(memory_space=pl.ANY)
    shapes = [((count,) + array.shape[1:], array.dtype) for array, _, count in jobs]
    sems = pltpu.SemaphoreType.DMA((len(jobs), pieces))
    return pl.pallas_call(
        functools.partial(cut_rows, counts, pieces),
        out_shape=[pltpu.HBM(*shape) for shape in shapes],
        in_specs=[pl.BlockSpec(memory_space=pltpu.SMEM)] + [anywhere] * len(jobs),
        out_specs=[anywhere] * len(jobs),
        scratch_shapes=[pltpu.VMEM(*shape) for shape in shapes] + [sems, sems],
        compiler_params=pltpu.CompilerParams(vmem_limit_bytes=8 * 2**20),
    )(
        jnp.stack([jnp.asarray(start, jnp.int32) for _, start, _ in jobs]),
        *[in_hbm(array) for array, _, _ in jobs],
    )


def share_columns(n_parts, column_ref, slab_ref, first_ref, *refs):
    parts, out_ref = refs[:n_parts], refs[n_parts]
    q, size, width = out_ref.shape[2:]
    pick = (
        lax.broadcasted_iota(jnp.int32, (size, width), 0)
        == lax.broadcasted_iota(jnp.int32, (size, width), 1) + column_ref[0]
    ).astype(jnp.bfloat16)
    for k, part in enumerate(parts):
        blocks = part.shape[0]
        rows = part[...].reshape(blocks * size, size)
        share = jnp.dot(rows, pick, preferred_element_type=jnp.float32)
        out_ref[slab_ref[k], pl.ds(first_ref[k], blocks // q)] = share.astype(
            out_ref.dtype
        ).reshape(blocks // q, q, size, width)


def call_share(parts, column, shape):
    smem = pl.BlockSpec(memory_space=pltpu.SMEM)
    vmem = pl.BlockSpec(memory_space=pltpu.VMEM)

    def numbers(k):
        return jnp.stack([jnp.asarray(part[k], jnp.int32) for part in parts])

    return pl.pallas_call(
        functools.partial(share_columns, len(parts)),
        out_shape=jax.ShapeDtypeStruct(shape, jnp.bfloat16),
        in_specs=[smem] * 3 + [vmem] * len(parts),
        out_specs=vmem,
        compiler_params=pltpu.CompilerParams(vmem_limit_bytes=16 * 2**20),
        cost_estimate=pl.CostEstimate(flops=10**9, bytes_accessed=2**22, transcendentals=0),
    )(
        jnp.asarray(column, jnp.int32).reshape(1), numbers(1), numbers(2),
        *[part[0] for part in parts],
    )


def store_residual(row, total, diag_ref, out_ref):
    size = total.shape[0]
    picks = total.shape[1] // size
    eye = (
        lax.broadcasted_iota(jnp.int32, (size, size), 0)
        == lax.broadcasted_iota(jnp.int32, (size, size), 1)
    ).astype(jnp.float32)
    for p in range(picks):
        on_diag = diag_ref[row * picks + p].astype(jnp.float32)
        block = total[:, p * size : (p + 1) * size] - on_diag * eye
        out_ref[row * picks + p] = block.astype(out_ref.dtype)


def store_scores(row, total, unused_ref, out_ref):
    size = total.shape[0]
    out_ref[pl.ds(row, 1), :] = jnp.sum(total * total, axis=0, keepdims=True) / size


def call_sums(a_pieces, tables, table_size, pick, extra, finish, out_shape, out_dtype):
    rows, slots, n_picks = pick.shape
    size = a_pieces[0].shape[-1]
    smem = pl.BlockSpec(memory_space=pltpu.SMEM)
    anywhere = pl.BlockSpec(memory_space=pl.ANY)
    flops = 2 * rows * slots * n_picks * size**3
    return pl.pallas_call(
        functools.partial(
            product_sums, len(a_pieces), [t.shape[0] for t, _ in tables], n_picks, finish
        ),
        out_shape=jax.ShapeDtypeStruct(out_shape, out_dtype),
        in_specs=[smem] * 3 + [anywhere] * (len(a_pieces) + len(tables)),
        out_specs=pl.BlockSpec(memory_space=pltpu.VMEM),
        scratch_shapes=[
            pltpu.VMEM((rows, slots, size, size), jnp.bfloat16),
            pltpu.VMEM((table_size + 1, size, size), jnp.bfloat16),
            pltpu.SemaphoreType.DMA((rows, len(a_pieces))),
            pltpu.SemaphoreType.DMA((len(tables),)),
        ],
        compiler_params=pltpu.CompilerParams(vmem_limit_bytes=18 * 2**20),
        cost_estimate=pl.CostEstimate(
            flops=flops, bytes_accessed=rows * slots * size * size * 4, transcendentals=0
        ),
    )(
        pick.reshape(-1).astype(jnp.int32),
        jnp.stack([jnp.asarray(start, jnp.int32) for _, start in tables]),
        extra.reshape(-1).astype(jnp.int32),
        *a_pieces,
        *[table for table, _ in tables],
    )


def on_device(acol, aval, mcol, mval, rpat, scol, cand):
    n_rows, n_blk = lax.axis_size("rows"), lax.axis_size("blk")
    rows_here, slots_here = acol.shape
    slabs, _, qm, size, _ = mval.shape
    q, c = rpat.shape[2], cand.shape[2]
    groups = n_blk // slabs
    group_rows = rows_here // groups
    total_rows = rows_here * n_rows
    i, j = lax.axis_index("rows"), lax.axis_index("blk")
    x, t = j // slabs, j % slabs
    own_row = x * group_rows

    def move(value, to):
        route = []
        for a in range(n_rows):
            for b in range(n_blk):
                ra, rx, rt = to(a, b // slabs, b % slabs)
                dest = (ra % n_rows) * n_blk + (rx % groups) * slabs + rt % slabs
                route.append((a * n_blk + b, dest))
        return lax.ppermute(value, ("rows", "blk"), route)

    def near_side(a, bx):
        return a + 1 if bx == 0 else a - 1

    def far_side(a, bx):
        return a - 1 if bx == 0 else a + 1

    m_flat = mval.reshape(-1, size, size)
    m_base = t * rows_here * qm
    block_m = group_rows * qm
    before, here, after = 0, rows_here, 2 * rows_here

    def wanted_by(dx):
        return ((x + dx) % groups) * group_rows

    m_own, *sent = call_cut(
        (m_flat, m_base, rows_here * qm),
        *[(aval, wanted_by(dx), group_rows) for dx in range(1, groups)],
    )
    a_far = [
        in_hbm(move(part, lambda a, bx, bt, dx=dx: (a, bx + dx, bt)))
        for dx, part in enumerate(sent, 1)
    ]
    m_tables = [(m_own, here * qm)]
    if groups == 2:
        half = group_rows // 2
        near = in_hbm(move(m_own, lambda a, bx, bt: (near_side(a, bx), bx, bt)))
        m_flat_then, aval_then, _ = lax.optimization_barrier((m_flat, aval, m_own))
        a_own, m_third = call_cut(
            (aval_then, own_row, group_rows),
            (m_flat_then, m_base + x * block_m + half * qm, block_m - half * qm),
        )
        m_third, near_part = lax.optimization_barrier((m_third, near))
        (near_part,) = call_cut((near_part, (1 - x) * block_m, half * qm))
        third = in_hbm(move(m_third, lambda a, bx, bt: (far_side(a, bx), bx, bt)))
        relayed = in_hbm(move(near_part, lambda a, bx, bt: (a, bx + 1, bt)))
        m_tables += [
            (near, jnp.where(x == 0, before, after) * qm),
            (third, jnp.where(x == 0, after, before + group_rows) * qm + half * qm),
            (relayed, jnp.where(x == 0, after, before + group_rows) * qm),
        ]
    else:
        (a_own,) = call_cut((aval, own_row, group_rows))
        m_tables += [
            (move(m_own, lambda a, bx, bt: (a + 1, bx, bt)), before * qm),
            (move(m_own, lambda a, bx, bt: (a - 1, bx, bt)), after * qm),
        ]

    def from_cores(value):
        return [value] + [
            in_hbm(move(value, lambda a, bx, bt, dt=dt: (a, bx, bt + dt)))
            for dt in range(1, slabs)
        ]

    a_pieces = []
    for piece in [a_own] + a_far:
        a_pieces += from_cores(piece)

    tags = jnp.concatenate([mcol, rpat], axis=2)
    if slabs == 2:
        one_side = move(tags, lambda a, bx, bt: (a + 1 if bt == 0 else a - 1, bx, bt))
    else:
        sides = [move(tags, lambda a, bx, bt, d=d: (a + d, bx, bt)) for d in (1, -1)]
    own_cols = [lax.dynamic_slice_in_dim(acol, own_row, group_rows, 0)] + [
        move(
            lax.dynamic_slice_in_dim(acol, wanted_by(dx), group_rows, 0),
            lambda a, bx, bt, dx=dx: (a, bx + dx, bt),
        )
        for dx in range(1, groups)
    ]
    own_cols = jnp.stack(own_cols, axis=1)
    if slabs == 2:
        flat = jnp.concatenate([own_cols.reshape(-1), one_side.reshape(-1)])
        other = move(flat, lambda a, bx, bt: (a, bx, bt + 1))
        cols = jnp.stack([own_cols, other[: own_cols.size].reshape(own_cols.shape)], axis=2)
        other_side = other[own_cols.size :].reshape(tags.shape)
        sides = [
            jnp.where(t == 0, one_side, other_side), jnp.where(t == 0, other_side, one_side)
        ]
    else:
        cols = jnp.stack(
            [own_cols]
            + [
                move(own_cols, lambda a, bx, bt, dt=dt: (a, bx, bt + dt))
                for dt in range(1, slabs)
            ],
            axis=2,
        )
    cols = cols.reshape(group_rows, -1)
    tags_ext = jnp.concatenate([sides[0], tags, sides[1]], axis=1)
    tags_ext = lax.dynamic_index_in_dim(tags_ext, t, 0, keepdims=False)
    present = cols >= 0
    position = jnp.where(present, (cols - i * rows_here + rows_here) % total_rows, 0)
    near_tags = tags_ext[position]
    pattern = lax.dynamic_slice(rpat, (t, own_row, 0), (1, group_rows, q))[0]
    wanted = lax.dynamic_slice(cand, (t, own_row, 0), (1, group_rows, c))[0]

    def picks(near, targets):
        width = near.shape[2]
        empty = 3 * rows_here * width
        hit = (near[:, :, :, None] == targets[:, None, None, :]) & present[:, :, None, None]
        at = position[:, :, None, None] * width + jnp.arange(width)[None, None, :, None]
        return empty + jnp.sum(jnp.where(hit, at - empty, 0), axis=2)

    m_pick = picks(near_tags[:, :, :qm], pattern)
    r_pick = picks(near_tags[:, :, qm:], wanted)
    slab_range = jnp.arange(scol.shape[1], dtype=jnp.int32)
    owner_row = lax.dynamic_index_in_dim(scol, t, 0, keepdims=False)
    owners = jnp.sum(
        jnp.where(pattern[:, :, None] == slab_range, owner_row[None, None, :], 0), axis=2
    )
    local_ids = i * rows_here + own_row + jnp.arange(group_rows, dtype=jnp.int32)
    on_diag = (owners == local_ids[:, None]).astype(jnp.int32)

    resid = call_sums(
        a_pieces, m_tables, 3 * rows_here * qm,
        m_pick, on_diag, store_residual,
        (group_rows * q, size, size), jnp.bfloat16,
    )

    block_r = group_rows * q
    if groups == 2:
        r_far = move(resid, lambda a, bx, bt: (far_side(a, bx), bx, bt))
        r_peer = move(resid, lambda a, bx, bt: (a, bx + 1, bt))
        r_next, r_far = lax.optimization_barrier((resid, r_far))
        r_near = move(r_next, lambda a, bx, bt: (near_side(a, bx), bx, bt))
        r_relay = move(r_far, lambda a, bx, bt: (a, bx + 1, bt))
        parts = [r_next, r_peer]
        r_tables = [
            (r_next, (here + own_row) * q),
            (in_hbm(r_peer), (here + (1 - x) * group_rows) * q),
            (in_hbm(r_near), jnp.where(x == 0, before, after + group_rows) * q),
            (in_hbm(r_far), jnp.where(x == 0, after, before + group_rows) * q),
            (in_hbm(r_relay), jnp.where(x == 0, before + group_rows, after) * q),
        ]
    else:
        parts = [resid]
        for dx in range(1, groups):
            parts.append(move(resid, lambda a, bx, bt, dx=dx: (a, bx + dx, bt)))
        order = (x - jnp.arange(groups)) % groups
        r_here = jnp.take(jnp.stack(parts), order, axis=0).reshape(-1, size, size)
        r_tables = [
            (r_here, here * q),
            (move(r_here, lambda a, bx, bt: (a + 1, bx, bt)), before * q),
            (move(r_here, lambda a, bx, bt: (a - 1, bx, bt)), after * q),
        ]

    width = size // n_blk
    shared = []
    for dx, part in enumerate(parts):
        for dt, moved in enumerate(from_cores(part)):
            shared.append((moved, (t - dt) % slabs, ((x - dx) % groups) * group_rows))
    resid_out = call_share(shared, j * width, (slabs, rows_here, q, size, width))
    r_pick, _ = lax.optimization_barrier((r_pick, resid_out))

    scores = call_sums(
        a_pieces, r_tables, 3 * rows_here * q,
        r_pick, on_diag, store_scores,
        (group_rows, c * size), jnp.float32,
    )
    gathered = lax.all_gather(scores.reshape(group_rows, c, size), "blk")
    gathered = lax.dynamic_slice_in_dim(gathered, j * width, width, 3)
    gathered = gathered.reshape(groups, slabs, group_rows, c, width)
    score_out = jnp.swapaxes(gathered, 0, 1).reshape(slabs, rows_here, c, width)
    return resid_out, score_out


def solution(mesh):
    placed = (
        P("rows", "blk"),
        P("rows", "blk", None, None),
        P(None, "rows", None),
        P(None, "rows", None, None, None),
        P(None, "rows", None),
        P(),
        P(None, "rows", None),
    )
    return jax.shard_map(
        on_device,
        mesh=mesh,
        in_specs=placed,
        out_specs=(P(None, "rows", None, None, "blk"), P(None, "rows", None, "blk")),
        check_vma=False,
    )
```

profile of v0, /device:TPU:0, one launch (start us, length us, event | category | flops | bytes accessed | tf_op | source)
XLA Modules:
  0.0 133.9 jit_solution(3681900519676780542)
XLA Ops:
  0.7 0.1 pad_add_fusion.7
  0.8 4.2 %shard_map.86 = (bf16[64,128,128]{2,1,0:T(8,128)(2,1)}, bf16[8,8,128,128]{3,2,1,0:T(8,128)(2,1)}) custom-call(s32[2]{0:T(128)S(1)} %get-tuple-element.47.start_ref, bf16[128,128,128]{2,1,0:T(8,128)(2,1)} %bitcast.46, bf16[16,8,128,128]{3,2,1,0:T(8,128)(2,1)} %refs_0_), custom_call_target="tpu_custom_call" | custom-call | tf_op jit(solution)/shard_map/pallas_call | solution.py:104
  5.0 3.0 %collective-permute-start.4 = (bf16[8,8,128,128]{3,2,1,0:T(8,128)(2,1)}, bf16[8,8,128,128]{3,2,1,0:T(8,128)(2,1)}, u32[]{:S(2)}, u32[]{:S(2)}) collective-permute-start(bf16[8,8,128,128]{3,2,1,0:T(8,128)(2,1)} %get-tuple-element.17), channel_id=1, source_target_pairs={{0,2},{1,3},{2,0},{3,1},{4,6},{5,7},{6,4},{7,5},{8,10},{9,11},{10,... | collective-permute-start | bytes 6291464 | tf_op jit(solution)/shard_map/ppermute | solution.py:222
  8.2 0.1 copy.134
  8.3 0.1 copy.135
  8.3 0.1 pad_add_fusion
  8.4 2.0 %collective-permute-start = (s32[2,16,6]{2,1,0:T(8,128)S(1)}, s32[2,16,6]{2,1,0:T(8,128)S(1)}, u32[]{:S(2)}, u32[]{:S(2)}) collective-permute-start(s32[2,16,6]{2,1,0:T(8,128)S(1)} %pad_add_fusion), channel_id=1, source_target_pairs={{0,4},{1,29},{2,6},{3,31},{4,8},{5,1},{6,10},{7,3},{8,12},{9,5},{1... | collective-permute-start | bytes 2312 | tf_op jit(solution)/shard_map/ppermute | solution.py:222
  10.4 1.5 %collective-permute-start.6 = (bf16[64,128,128]{2,1,0:T(8,128)(2,1)}, bf16[64,128,128]{2,1,0:T(8,128)(2,1)}, u32[]{:S(2)}, u32[]{:S(2)}) collective-permute-start(bf16[64,128,128]{2,1,0:T(8,128)(2,1)} %get-tuple-element.13.refs_4_), channel_id=1, source_target_pairs={{0,4},{1,5},{2,30},{3,31},{4,8},{5,9},{6,2},{7,3},{8,12},{9,13},{1... | collective-permute-start | bytes 6291464 | tf_op jit(solution)/shard_map/ppermute | solution.py:222
  12.0 3.2 %shard_map.87 = (bf16[8,8,128,128]{3,2,1,0:T(8,128)(2,1)}, bf16[16,128,128]{2,1,0:T(8,128)(2,1)}) custom-call(s32[2]{0:T(128)S(1)} %get-tuple-element.46.start_ref, bf16[16,8,128,128]{3,2,1,0:T(8,128)(2,1)} %refs_0_, bf16[128,128,128]{2,1,0:T(8,128)(2,1)} %bitcast.47), custom_call_target="tpu_custom_call" | custom-call | tf_op jit(solution)/shard_map/pallas_call | solution.py:104
  15.2 0.6 collective-permute-start.3
  15.8 0.1 fusion.7
  15.8 0.2 select_reduce_fusion.2
  16.1 37.9 %collective-permute-done.4.refs_2_ = bf16[8,8,128,128]{3,2,1,0:T(8,128)(2,1)} collective-permute-done((bf16[8,8,128,128]{3,2,1,0:T(8,128)(2,1)}, bf16[8,8,128,128]{3,2,1,0:T(8,128)(2,1)}, u32[]{:S(2)}, u32[]{:S(2)}) %collective-permute-start.4) | collective-permute-done | bytes 2097184 | tf_op jit(solution)/shard_map/ppermute | solution.py:222
  54.1 0.1 reshape.191
  54.2 0.1 reshape.192
  54.3 0.6 collective-permute-start.2
  54.9 0.1 pad_add_fusion.6.start_ref
  54.9 0.1 copy.140
  55.0 0.1 copy.156
  55.1 0.1 reshape.198.extra_ref
  55.2 2.9 %collective-permute-done.2 = s32[320]{0:T(512)S(1)} collective-permute-done((s32[320]{0:T(512)S(1)}, s32[320]{0:T(512)S(1)}, u32[]{:S(2)}, u32[]{:S(2)}) %collective-permute-start.2) | collective-permute-done | bytes 1312 | tf_op jit(solution)/shard_map/ppermute | solution.py:222
  58.1 0.1 stack_reshape.3
  58.4 0.1 copy.144
  58.4 0.1 copy.152
  58.5 0.1 reshape.193
  58.7 0.1 copy.141
  58.7 0.1 copy.139
  58.8 0.1 add.217
  59.0 0.1 reshape.201
  59.1 0.1 fusion.6
  59.2 0.1 copy.142
  59.3 0.7 gather_fusion
  60.0 0.1 copy.150
  60.1 0.7 collective-permute-done.6.refs_0_.refs_5_
  60.9 1.8 %shard_map.88 = bf16[16,128,128]{2,1,0:T(8,128)(2,1)} custom-call(s32[1]{0:T(128)} %bitcast.23.start_ref, bf16[64,128,128]{2,1,0:T(8,128)(2,1)} %collective-permute-done.6.refs_0_.refs_5_), custom_call_target="tpu_custom_call" | custom-call | tf_op jit(solution)/shard_map/pallas_call | solution.py:104
  62.7 1.1 collective-permute-start.8
  63.8 4.6 %collective-permute-start.7 = (bf16[16,128,128]{2,1,0:T(8,128)(2,1)}, bf16[16,128,128]{2,1,0:T(8,128)(2,1)}, u32[]{:S(2)}, u32[]{:S(2)}) collective-permute-start(bf16[16,128,128]{2,1,0:T(8,128)(2,1)} %get-tuple-element.19), channel_id=1, source_target_pairs={{0,28},{1,29},{2,6},{3,7},{4,0},{5,1},{6,10},{7,11},{8,4},{9,5},{1... | collective-permute-start | bytes 1572872 | tf_op jit(solution)/shard_map/ppermute | solution.py:222
  68.3 0.1 select_reduce_fusion
  68.4 0.1 copy.155
  68.6 0.1 add.224.pick_ref
  68.7 9.0 %collective-permute-done.8.refs_7_ = bf16[16,128,128]{2,1,0:T(8,128)(2,1)S(1)} collective-permute-done((bf16[16,128,128]{2,1,0:T(8,128)(2,1)}, bf16[16,128,128]{2,1,0:T(8,128)(2,1)S(1)}, u32[]{:S(2)}, u32[]{:S(2)}) %collective-permute-start.8) | collective-permute-done | bytes 524320 | tf_op jit(solution)/shard_map/ppermute | solution.py:222
  77.7 2.2 %collective-permute-done.7.refs_6_ = bf16[16,128,128]{2,1,0:T(8,128)(2,1)} collective-permute-done((bf16[16,128,128]{2,1,0:T(8,128)(2,1)}, bf16[16,128,128]{2,1,0:T(8,128)(2,1)}, u32[]{:S(2)}, u32[]{:S(2)}) %collective-permute-start.7) | collective-permute-done | bytes 524320 | tf_op jit(solution)/shard_map/ppermute | solution.py:222
  79.9 1.6 %copy-done.4 = bf16[64,128,128]{2,1,0:T(8,128)(2,1)S(1)} copy-done((bf16[64,128,128]{2,1,0:T(8,128)(2,1)S(1)}, bf16[64,128,128]{2,1,0:T(8,128)(2,1)}, u32[]{:S(2)}) %copy-start.4) | copy-done | bytes 2097176
  81.5 6.7 %shard_map.89.refs_0_.refs_4_ = bf16[16,128,128]{2,1,0:T(8,128)(2,1)S(1)} custom-call(s32[512]{0:T(512)S(1)} %add.224.pick_ref, s32[4]{0:T(128)S(1)} %pad_add_fusion.6.start_ref, s32[16]{0:T(128)S(1)} %reshape.198.extra_ref, bf16[8,8,128,128]{3,2,1,0:T(8,128)(2,1)S(1)} %copy-done.1, bf16[8,8,128,128]{3,2,1,0:T(8,128)(2,1)} %collective-permute-done.3.refs_1_, ...), custom_call_target="tpu_custom_call" | custom-call | flops 2147483648 | bytes 16777216 | tf_op jit(solution)/shard_map/pallas_call | solution.py:177
  88.1 5.2 %collective-permute-start.9 = (bf16[16,128,128]{2,1,0:T(8,128)(2,1)S(1)}, bf16[16,128,128]{2,1,0:T(8,128)(2,1)}, u32[]{:S(2)}, u32[]{:S(2)}) collective-permute-start(bf16[16,128,128]{2,1,0:T(8,128)(2,1)S(1)} %shard_map.89.refs_0_.refs_4_), channel_id=1, source_target_pairs={{0,28},{1,29},{2,6},{3,7},{4,0},{5,1},{6,10},{7,11},{8,4},{9,5},{1... | collective-permute-start | bytes 1572872 | tf_op jit(solution)/shard_map/ppermute | solution.py:222
  93.4 0.1 stack.115.start_ref
  93.6 10.1 %collective-permute-done.9.refs_7_ = bf16[16,128,128]{2,1,0:T(8,128)(2,1)} collective-permute-done((bf16[16,128,128]{2,1,0:T(8,128)(2,1)S(1)}, bf16[16,128,128]{2,1,0:T(8,128)(2,1)}, u32[]{:S(2)}, u32[]{:S(2)}) %collective-permute-start.9) | collective-permute-done | bytes 524320 | tf_op jit(solution)/shard_map/ppermute | solution.py:222
  103.7 3.3 %collective-permute-start.14 = (bf16[16,128,128]{2,1,0:T(8,128)(2,1)}, bf16[16,128,128]{2,1,0:T(8,128)(2,1)}, u32[]{:S(2)}, u32[]{:S(2)}) collective-permute-start(bf16[16,128,128]{2,1,0:T(8,128)(2,1)} %collective-permute-done.9.refs_7_), channel_id=1, source_target_pairs={{0,2},{1,3},{2,0},{3,1},{4,6},{5,7},{6,4},{7,5},{8,10},{9,11},{10,... | collective-permute-start | bytes 1572872 | tf_op jit(solution)/shard_map/ppermute | solution.py:222
  107.1 0.2 collective-permute-start.12
  107.3 0.1 slice.27
  107.4 0.1 copy.157
  107.5 0.1 select_reduce_fusion.1
  107.6 1.4 %collective-permute-done.12.refs_3_ = bf16[16,128,128]{2,1,0:T(8,128)(2,1)S(1)} collective-permute-done((bf16[16,128,128]{2,1,0:T(8,128)(2,1)S(1)}, bf16[16,128,128]{2,1,0:T(8,128)(2,1)S(1)}, u32[]{:S(2)}, u32[]{:S(2)}) %collective-permute-start.12) | collective-permute-done | bytes 524320 | tf_op jit(solution)/shard_map/ppermute | solution.py:222
  109.0 0.8 copy-done.6
  109.8 0.1 copy-done.5
  109.9 2.1 %shard_map.90 = bf16[2,16,2,128,32]{4,3,2,1,0:T(8,128)(2,1)S(1)} custom-call(s32[1]{0:T(128)} %bitcast.column_ref, s32[4]{0:T(128)S(1)} %get-tuple-element.44.slab_ref, s32[4]{0:T(128)S(1)} %get-tuple-element.45.first_ref, bf16[16,128,128]{2,1,0:T(8,128)(2,1)S(1)} %shard_map.89.refs_0_.refs_4_, bf16[16,128,128]{2,1,0:T(8,128)(2,1)} %copy-done.5, ...), custom_call_target="tpu_custom_call" | custom-call | flops 1000000000 | bytes 4194304 | tf_op jit(solution)/shard_map/pallas_call | solution.py:140
  112.0 1.5 %copy.161 = bf16[2,16,2,128,32]{3,4,2,1,0:T(8,128)(2,1)} copy(bf16[2,16,2,128,32]{4,3,2,1,0:T(8,128)(2,1)S(1)} %shard_map.90) | data formatting | bytes 1048576
  113.5 0.1 copy.159
  113.6 0.1 reshape.195.pick_ref
  113.8 6.2 %collective-permute-done.14.refs_8_ = bf16[16,128,128]{2,1,0:T(8,128)(2,1)} collective-permute-done((bf16[16,128,128]{2,1,0:T(8,128)(2,1)}, bf16[16,128,128]{2,1,0:T(8,128)(2,1)}, u32[]{:S(2)}, u32[]{:S(2)}) %collective-permute-start.14) | collective-permute-done | bytes 524320 | tf_op jit(solution)/shard_map/ppermute | solution.py:222
  120.0 1.6 %copy-done.2 = bf16[8,8,128,128]{3,2,1,0:T(8,128)(2,1)S(1)} copy-done((bf16[8,8,128,128]{3,2,1,0:T(8,128)(2,1)S(1)}, bf16[8,8,128,128]{3,2,1,0:T(8,128)(2,1)}, u32[]{:S(2)}) %copy-start.2) | copy-done | bytes 2097176
  121.6 6.4 %shard_map.91 = f32[8,256]{1,0:T(8,128)S(1)} custom-call(s32[512]{0:T(512)S(1)} %reshape.195.pick_ref, s32[5]{0:T(128)S(1)} %stack.115.start_ref, s32[16]{0:T(128)S(1)} %reshape.198.extra_ref, bf16[8,8,128,128]{3,2,1,0:T(8,128)(2,1)S(1)} %copy-done.2, bf16[8,8,128,128]{3,2,1,0:T(8,128)(2,1)} %collective-permute-done.3.refs_1_, ...), custom_call_target="tpu_custom_call" | custom-call | flops 2147483648 | bytes 16777216 | tf_op jit(solution)/shard_map/pallas_call | solution.py:177
  128.0 5.2 %all_gather.3 = f32[4,8,2,128]{3,1,2,0:T(8,128)S(1)} all-gather(f32[1,8,2,128]{3,1,2,0:T(8,128)S(1)} %bitcast.44), channel_id=1, replica_groups=mesh['rows'=8,'blk'=4] {'blk'}, dimensions={0}, use_global_device_ids=true | all-gather | bytes 40960 | tf_op jit(solution)/shard_map/all_gather | solution.py:383
  133.2 0.6 copy.162
  (61 shorter events, 0.8 us)
Async XLA Ops:
  0.6 92.8 %copy-start = (s32[2,16,2]{1,2,0:T(2,128)S(1)}, s32[2,16,2]{1,2,0:T(2,128)}, u32[]{:S(2)}) copy-start(s32[2,16,2]{1,2,0:T(2,128)} %param.13) | copy-start | bytes 772
  0.8 7.2 %copy-start.8 = (s32[16,8]{0,1:T(8,128)S(1)}, s32[16,8]{0,1:T(8,128)}, u32[]{:S(2)}) copy-start(s32[16,8]{0,1:T(8,128)} %param.7) | copy-start | bytes 1540
  0.8 7.4 %copy-start.10 = (s32[2,16,4]{1,2,0:T(4,128)S(1)}, s32[2,16,4]{1,2,0:T(4,128)}, u32[]{:S(2)}) copy-start(s32[2,16,4]{1,2,0:T(4,128)} %param.9) | copy-start | bytes 1540
  0.8 7.5 %copy-start.9 = (s32[2,16,2]{1,2,0:T(2,128)S(1)}, s32[2,16,2]{1,2,0:T(2,128)}, u32[]{:S(2)}) copy-start(s32[2,16,2]{1,2,0:T(2,128)} %param.11) | copy-start | bytes 772
  5.0 49.0 %collective-permute-start.4 = (bf16[8,8,128,128]{3,2,1,0:T(8,128)(2,1)}, bf16[8,8,128,128]{3,2,1,0:T(8,128)(2,1)}, u32[]{:S(2)}, u32[]{:S(2)}) collective-permute-start(bf16[8,8,128,128]{3,2,1,0:T(8,128)(2,1)} %get-tuple-element.17), channel_id=1, source_target_pairs={{0,2},{1,3},{2,0},{3,1},{4,6},{5,7},{6,4},{7,5},{8,10},{9,11},{10,... | collective-permute-start | bytes 6291464 | tf_op jit(solution)/shard_map/ppermute | solution.py:222
  8.1 45.9 %collective-permute-start.1 = (s32[8,8]{1,0:T(8,128)S(1)}, s32[8,8]{1,0:T(8,128)S(1)}, u32[]{:S(2)}, u32[]{:S(2)}) collective-permute-start(s32[8,8]{1,0:T(8,128)S(1)} %copy.166), channel_id=1, source_target_pairs={{0,2},{1,3},{2,0},{3,1},{4,6},{5,7},{6,4},{7,5},{8,10},{9,11},{10,... | collective-permute-start | bytes 776 | tf_op jit(solution)/shard_map/ppermute | solution.py:222
  8.4 45.7 %collective-permute-start = (s32[2,16,6]{2,1,0:T(8,128)S(1)}, s32[2,16,6]{2,1,0:T(8,128)S(1)}, u32[]{:S(2)}, u32[]{:S(2)}) collective-permute-start(s32[2,16,6]{2,1,0:T(8,128)S(1)} %pad_add_fusion), channel_id=1, source_target_pairs={{0,4},{1,29},{2,6},{3,31},{4,8},{5,1},{6,10},{7,3},{8,12},{9,5},{1... | collective-permute-start | bytes 2312 | tf_op jit(solution)/shard_map/ppermute | solution.py:222
  10.4 50.4 %collective-permute-start.6 = (bf16[64,128,128]{2,1,0:T(8,128)(2,1)}, bf16[64,128,128]{2,1,0:T(8,128)(2,1)}, u32[]{:S(2)}, u32[]{:S(2)}) collective-permute-start(bf16[64,128,128]{2,1,0:T(8,128)(2,1)} %get-tuple-element.13.refs_4_), channel_id=1, source_target_pairs={{0,4},{1,5},{2,30},{3,31},{4,8},{5,9},{6,2},{7,3},{8,12},{9,13},{1... | collective-permute-start | bytes 6291464 | tf_op jit(solution)/shard_map/ppermute | solution.py:222
  12.0 3.8 %copy-start.11 = (s32[2,64]{1,0:T(2,128)S(1)}, s32[2,64]{1,0:T(2,128)}, u32[]{:S(2)}) copy-start(s32[2,64]{1,0:T(2,128)} %param.12) | copy-start | bytes 1540
  15.2 53.5 %collective-permute-start.3 = (bf16[8,8,128,128]{3,2,1,0:T(8,128)(2,1)}, bf16[8,8,128,128]{3,2,1,0:T(8,128)(2,1)}, u32[]{:S(2)}, u32[]{:S(2)}) collective-permute-start(bf16[8,8,128,128]{3,2,1,0:T(8,128)(2,1)} %get-tuple-element.16.refs_0_), channel_id=1, source_target_pairs={{0,1},{1,0},{2,3},{3,2},{4,5},{5,4},{6,7},{7,6},{8,9},{9,8},{10,11... | collective-permute-start | bytes 6291464 | tf_op jit(solution)/shard_map/ppermute | solution.py:222
  54.0 25.9 %collective-permute-start.5 = (bf16[8,8,128,128]{3,2,1,0:T(8,128)(2,1)}, bf16[8,8,128,128]{3,2,1,0:T(8,128)(2,1)}, u32[]{:S(2)}, u32[]{:S(2)}) collective-permute-start(bf16[8,8,128,128]{3,2,1,0:T(8,128)(2,1)} %collective-permute-done.4.refs_2_), channel_id=1, source_target_pairs={{0,1},{1,0},{2,3},{3,2},{4,5},{5,4},{6,7},{7,6},{8,9},{9,8},{10,11... | collective-permute-start | bytes 6291464 | tf_op jit(solution)/shard_map/ppermute | solution.py:222
  54.3 3.8 %collective-permute-start.2 = (s32[320]{0:T(512)S(1)}, s32[320]{0:T(512)S(1)}, u32[]{:S(2)}, u32[]{:S(2)}) collective-permute-start(s32[320]{0:T(512)S(1)} %pad_add_fusion.3), channel_id=1, source_target_pairs={{0,1},{1,0},{2,3},{3,2},{4,5},{5,4},{6,7},{7,6},{8,9},{9,8},{10,11... | collective-permute-start | bytes 3848 | tf_op jit(solution)/shard_map/ppermute | solution.py:222
  59.3 20.6 %copy-start.1 = (bf16[8,8,128,128]{3,2,1,0:T(8,128)(2,1)S(1)}, bf16[8,8,128,128]{3,2,1,0:T(8,128)(2,1)}, u32[]{:S(2)}) copy-start(bf16[8,8,128,128]{3,2,1,0:T(8,128)(2,1)} %get-tuple-element.16.refs_0_) | copy-start | bytes 6291460
  62.7 15.0 %collective-permute-start.8 = (bf16[16,128,128]{2,1,0:T(8,128)(2,1)}, bf16[16,128,128]{2,1,0:T(8,128)(2,1)S(1)}, u32[]{:S(2)}, u32[]{:S(2)}) collective-permute-start(bf16[16,128,128]{2,1,0:T(8,128)(2,1)} %shard_map.88), channel_id=1, source_target_pairs={{0,2},{1,3},{2,0},{3,1},{4,6},{5,7},{6,4},{7,5},{8,10},{9,11},{10,... | collective-permute-start | bytes 1572872 | tf_op jit(solution)/shard_map/ppermute | solution.py:222
  63.8 16.1 %collective-permute-start.7 = (bf16[16,128,128]{2,1,0:T(8,128)(2,1)}, bf16[16,128,128]{2,1,0:T(8,128)(2,1)}, u32[]{:S(2)}, u32[]{:S(2)}) collective-permute-start(bf16[16,128,128]{2,1,0:T(8,128)(2,1)} %get-tuple-element.19), channel_id=1, source_target_pairs={{0,28},{1,29},{2,6},{3,7},{4,0},{5,1},{6,10},{7,11},{8,4},{9,5},{1... | collective-permute-start | bytes 1572872 | tf_op jit(solution)/shard_map/ppermute | solution.py:222
  77.7 2.2 %copy-start.7 = (bf16[16,128,128]{2,1,0:T(8,128)(2,1)}, bf16[16,128,128]{2,1,0:T(8,128)(2,1)S(1)}, u32[]{:S(2)}) copy-start(bf16[16,128,128]{2,1,0:T(8,128)(2,1)S(1)} %collective-permute-done.8.refs_7_) | copy-start | bytes 1572868
  79.9 1.6 %copy-start.4 = (bf16[64,128,128]{2,1,0:T(8,128)(2,1)S(1)}, bf16[64,128,128]{2,1,0:T(8,128)(2,1)}, u32[]{:S(2)}) copy-start(bf16[64,128,128]{2,1,0:T(8,128)(2,1)} %get-tuple-element.13.refs_4_) | copy-start | bytes 6291460
  88.1 15.6 %collective-permute-start.9 = (bf16[16,128,128]{2,1,0:T(8,128)(2,1)S(1)}, bf16[16,128,128]{2,1,0:T(8,128)(2,1)}, u32[]{:S(2)}, u32[]{:S(2)}) collective-permute-start(bf16[16,128,128]{2,1,0:T(8,128)(2,1)S(1)} %shard_map.89.refs_0_.refs_4_), channel_id=1, source_target_pairs={{0,28},{1,29},{2,6},{3,7},{4,0},{5,1},{6,10},{7,11},{8,4},{9,5},{1... | collective-permute-start | bytes 1572872 | tf_op jit(solution)/shard_map/ppermute | solution.py:222
  93.4 13.7 %collective-permute-start.11 = (bf16[16,128,128]{2,1,0:T(8,128)(2,1)S(1)}, bf16[16,128,128]{2,1,0:T(8,128)(2,1)S(1)}, u32[]{:S(2)}, u32[]{:S(2)}) collective-permute-start(bf16[16,128,128]{2,1,0:T(8,128)(2,1)S(1)} %shard_map.89.refs_0_.refs_4_), channel_id=1, source_target_pairs={{0,2},{1,3},{2,0},{3,1},{4,6},{5,7},{6,4},{7,5},{8,10},{9,11},{10,... | collective-permute-start | bytes 1572872 | tf_op jit(solution)/shard_map/ppermute | solution.py:222
  103.7 16.3 %collective-permute-start.13 = (bf16[16,128,128]{2,1,0:T(8,128)(2,1)S(1)}, bf16[16,128,128]{2,1,0:T(8,128)(2,1)}, u32[]{:S(2)}, u32[]{:S(2)}) collective-permute-start(bf16[16,128,128]{2,1,0:T(8,128)(2,1)S(1)} %shard_map.89.refs_0_.refs_4_), channel_id=1, source_target_pairs={{0,4},{1,5},{2,30},{3,31},{4,8},{5,9},{6,2},{7,3},{8,12},{9,13},{1... | collective-permute-start | bytes 1572872 | tf_op jit(solution)/shard_map/ppermute | solution.py:222
  103.7 5.3 %collective-permute-start.10 = (bf16[16,128,128]{2,1,0:T(8,128)(2,1)S(1)}, bf16[16,128,128]{2,1,0:T(8,128)(2,1)S(1)}, u32[]{:S(2)}, u32[]{:S(2)}) collective-permute-start(bf16[16,128,128]{2,1,0:T(8,128)(2,1)S(1)} %shard_map.89.refs_0_.refs_4_), channel_id=1, source_target_pairs={{0,1},{1,0},{2,3},{3,2},{4,5},{5,4},{6,7},{7,6},{8,9},{9,8},{10,11... | collective-permute-start | bytes 1572872 | tf_op jit(solution)/shard_map/ppermute | solution.py:222
  103.7 16.3 %collective-permute-start.14 = (bf16[16,128,128]{2,1,0:T(8,128)(2,1)}, bf16[16,128,128]{2,1,0:T(8,128)(2,1)}, u32[]{:S(2)}, u32[]{:S(2)}) collective-permute-start(bf16[16,128,128]{2,1,0:T(8,128)(2,1)} %collective-permute-done.9.refs_7_), channel_id=1, source_target_pairs={{0,2},{1,3},{2,0},{3,1},{4,6},{5,7},{6,4},{7,5},{8,10},{9,11},{10,... | collective-permute-start | bytes 1572872 | tf_op jit(solution)/shard_map/ppermute | solution.py:222
  107.1 4.9 %copy-start.3 = (bf16[16,128,128]{2,1,0:T(8,128)(2,1)}, bf16[16,128,128]{2,1,0:T(8,128)(2,1)S(1)}, u32[]{:S(2)}) copy-start(bf16[16,128,128]{2,1,0:T(8,128)(2,1)S(1)} %collective-permute-done.11.refs_2_.refs_5_) | copy-start | bytes 1572868
  107.1 1.9 %collective-permute-start.12 = (bf16[16,128,128]{2,1,0:T(8,128)(2,1)S(1)}, bf16[16,128,128]{2,1,0:T(8,128)(2,1)S(1)}, u32[]{:S(2)}, u32[]{:S(2)}) collective-permute-start(bf16[16,128,128]{2,1,0:T(8,128)(2,1)S(1)} %collective-permute-done.11.refs_2_.refs_5_), channel_id=1, source_target_pairs={{0,1},{1,0},{2,3},{3,2},{4,5},{5,4},{6,7},{7,6},{8,9},{9,8},{10,11... | collective-permute-start | bytes 1572872 | tf_op jit(solution)/shard_map/ppermute | solution.py:222
  109.0 0.8 copy-start.6
  109.0 1.0 copy-start.5
  120.0 1.6 %copy-start.2 = (bf16[8,8,128,128]{3,2,1,0:T(8,128)(2,1)S(1)}, bf16[8,8,128,128]{3,2,1,0:T(8,128)(2,1)}, u32[]{:S(2)}) copy-start(bf16[8,8,128,128]{3,2,1,0:T(8,128)(2,1)} %get-tuple-element.16.refs_0_) | copy-start | bytes 6291460
where the time goes:
time: 134 us
  waiting for transfers between devices  70.4 us (53%)
  Pallas kernels  24.3 us (18%)
  starting transfers between devices  22.2 us (17%)
  local copies, waits for them, and re-layouts  10 us (7%)
  blocking collectives  5.19 us (4%)
    ppermute x15, waiting for transfers between devices, move(): return lax.ppermute(value, ('rows', 'blk'), route)  70.4 us
    ppermute x15, starting transfers between devices, move(): return lax.ppermute(value, ('rows', 'blk'), route)  22.2 us
    pallas_call x2, Pallas kernels, call_sums(): pl.pallas_call(functools.partial(product_sums, len(a_pieces), [t.shape[0]...  13.1 us
    pallas_call x3, Pallas kernels, call_cut(): pl.pallas_call(functools.partial(cut_rows, counts, pieces), out_shape=[pl...  9.19 us
    unnamed x30, local copies, waits for them, and re-layouts  6.64 us
    all_gather x1, blocking collectives, on_device(): gathered = lax.all_gather(scores.reshape(group_rows, c, size), 'blk')  5.19 us
  transfers between devices with their start and end apart: 15, of which 8 were waited for; matrix products, arithmetic and copies ran while one was open for 4% of the time, Pallas kernels for 5%

commit v1 on v0

v1 whole, which is shorter than its diff:
```python
import functools

import jax
import jax.numpy as jnp
from jax import lax
from jax.experimental import pallas as pl
from jax.experimental.pallas import tpu as pltpu
from jax.sharding import PartitionSpec as P


def table_copies(ranges, sources, start_ref, tab, sems):
    return [
        pltpu.make_async_copy(
            source.at[pl.ds(first, count)], tab.at[pl.ds(start_ref[k], count)], sems.at[k]
        )
        for k, (source, (first, count)) in enumerate(zip(sources, ranges))
    ]


def row_sum(total, row, slots, block, tab, pick_ref, n_picks):
    for slot in range(0, slots, 2):
        left = jnp.concatenate([block(row, slot), block(row, slot + 1)], axis=1)
        at = (row * slots + slot) * n_picks
        right = jnp.concatenate(
            [
                jnp.concatenate(
                    [tab[pick_ref[at + k * n_picks + p]] for p in range(n_picks)], axis=1
                )
                for k in range(2)
            ],
            axis=0,
        )
        total += jnp.dot(left, right, preferred_element_type=jnp.float32)
    return total


def all_slots(t_counts, n_picks, finish, pick_ref, start_ref, after_ref, extra_ref, a_ref, *refs):
    t_refs, out_ref = refs[: len(t_counts)], refs[len(t_counts)]
    tab, t_sems = refs[len(t_counts) + 1 :]
    rows, slots, size = a_ref.shape[:3]
    tables = table_copies(t_counts, t_refs, start_ref, tab, t_sems)
    for copy in tables:
        copy.start()
    tab[tab.shape[0] - 1] = jnp.zeros(tab.shape[1:], tab.dtype)
    for copy in tables:
        copy.wait()

    def block(row, slot):
        return a_ref[row, slot]

    def one_row(row, carry):
        total = jnp.zeros((size, n_picks * size), jnp.float32)
        total = row_sum(total, row, slots, block, tab, pick_ref, n_picks)
        finish(row, total, extra_ref, out_ref)
        return carry

    lax.fori_loop(0, rows, one_row, 0)


def join_pieces(n_pieces, first_ref, *refs):
    pieces, out_ref, sems = refs[:n_pieces], refs[n_pieces], refs[n_pieces + 1]
    rows, width = out_ref.shape[0], out_ref.shape[1] // n_pieces
    copies = []
    for k, piece in enumerate(pieces):
        first = 0 if piece.shape[0] == rows else first_ref[0]
        copies.append(
            pltpu.make_async_copy(
                piece.at[pl.ds(first, rows)], out_ref.at[:, pl.ds(k * width, width)], sems.at[k]
            )
        )
    for copy in copies:
        copy.start()
    for copy in copies:
        copy.wait()


def call_join(pieces, first, rows):
    slots, size = pieces[0].shape[1:3]
    anywhere = pl.BlockSpec(memory_space=pl.ANY)
    return pl.pallas_call(
        functools.partial(join_pieces, len(pieces)),
        out_shape=pltpu.VMEM((rows, slots * len(pieces), size, size), pieces[0].dtype),
        in_specs=[pl.BlockSpec(memory_space=pltpu.SMEM)] + [anywhere] * len(pieces),
        out_specs=anywhere,
        scratch_shapes=[pltpu.SemaphoreType.DMA((len(pieces),))],
        compiler_params=pltpu.CompilerParams(vmem_limit_bytes=2**20),
        cost_estimate=pl.CostEstimate(flops=10**9, bytes_accessed=2**24, transcendentals=0),
    )(jnp.asarray(first, jnp.int32).reshape(1), in_hbm(pieces[0]), *pieces[1:])


def cut_rows(counts, pieces, start_ref, turn_ref, *refs):
    n = len(counts)
    sources, outs, token_ref = refs[:n], refs[n : 2 * n], refs[2 * n]
    stages, (in_sems, out_sems) = refs[2 * n + 1 : 3 * n + 1], refs[3 * n + 1 :]
    token_ref[0] = 0

    def copy_in(k, p):
        size = counts[k] // pieces
        return pltpu.make_async_copy(
            sources[k].at[pl.ds(start_ref[k] + lax.rem(p + turn_ref[k], pieces) * size, size)],
            stages[k].at[pl.ds(p * size, size)],
            in_sems.at[k, p],
        )

    def copy_out(k, p):
        part = pl.ds(p * (counts[k] // pieces), counts[k] // pieces)
        return pltpu.make_async_copy(stages[k].at[part], outs[k].at[part], out_sems.at[k, p])

    every = [(k, p) for k in range(n) for p in range(pieces)]
    for k, p in every:
        copy_in(k, p).start()
    for k, p in every:
        copy_in(k, p).wait()
        copy_out(k, p).start()
    for k, p in every:
        copy_out(k, p).wait()


def in_hbm(array):
    return pltpu.with_memory_space_constraint(array, pltpu.HBM)


def call_cut(jobs, flops=10**9):
    counts = [job[2] for job in jobs]
    pieces = 4
    smem = pl.BlockSpec(memory_space=pltpu.SMEM)
    anywhere = pl.BlockSpec(memory_space=pl.ANY)
    shapes = [((job[2],) + job[0].shape[1:], job[0].dtype) for job in jobs]
    sems = pltpu.SemaphoreType.DMA((len(jobs), pieces))
    return pl.pallas_call(
        functools.partial(cut_rows, counts, pieces),
        out_shape=[pltpu.HBM(*shape) for shape in shapes]
        + [jax.ShapeDtypeStruct((1,), jnp.int32)],
        in_specs=[smem] * 2 + [anywhere] * len(jobs),
        out_specs=[anywhere] * len(jobs) + [smem],
        scratch_shapes=[pltpu.VMEM(*shape) for shape in shapes] + [sems, sems],
        compiler_params=pltpu.CompilerParams(vmem_limit_bytes=8 * 2**20),
        cost_estimate=pl.CostEstimate(flops=flops, bytes_accessed=2**22, transcendentals=0),
    )(
        flat_numbers([job[1] for job in jobs]),
        flat_numbers([job[3] for job in jobs]),
        *[job[0] for job in jobs],
    )


def share_columns(n_parts, column_ref, slab_ref, first_ref, *refs):
    parts, (out_ref, done_ref) = refs[:n_parts], refs[n_parts:]
    q, width, size = out_ref.shape[2:]
    done_ref[0] = 0
    pick = (
        lax.broadcasted_iota(jnp.int32, (width, size), 1)
        == lax.broadcasted_iota(jnp.int32, (width, size), 0) + column_ref[0]
    ).astype(jnp.bfloat16)
    for k, part in enumerate(parts):
        blocks = part.shape[0]
        rows = part[...].reshape(blocks * size, size)
        share = lax.dot_general(
            pick, rows, (((1,), (1,)), ((), ())), preferred_element_type=jnp.float32
        ).astype(out_ref.dtype)
        for n in range(blocks):
            out_ref[slab_ref[k], first_ref[k] + n // q, n % q] = share[
                :, n * size : (n + 1) * size
            ]


def call_share(parts, column, shape):
    smem = pl.BlockSpec(memory_space=pltpu.SMEM)
    vmem = pl.BlockSpec(memory_space=pltpu.VMEM)

    def numbers(k):
        return jnp.stack([jnp.asarray(part[k], jnp.int32) for part in parts])

    return pl.pallas_call(
        functools.partial(share_columns, len(parts)),
        out_shape=[
            jax.ShapeDtypeStruct(shape, jnp.bfloat16), jax.ShapeDtypeStruct((1,), jnp.int32)
        ],
        in_specs=[smem] * 3 + [vmem] * len(parts),
        out_specs=[vmem, smem],
        compiler_params=pltpu.CompilerParams(vmem_limit_bytes=6 * 2**20),
        cost_estimate=pl.CostEstimate(flops=10**9, bytes_accessed=2**22, transcendentals=0),
    )(
        jnp.asarray(column, jnp.int32).reshape(1), numbers(1), numbers(2),
        *[part[0] for part in parts],
    )


def store_residual(row, total, diag_ref, out_ref):
    size = total.shape[0]
    picks = total.shape[1] // size
    eye = (
        lax.broadcasted_iota(jnp.int32, (size, size), 0)
        == lax.broadcasted_iota(jnp.int32, (size, size), 1)
    ).astype(jnp.float32)
    for p in range(picks):
        on_diag = diag_ref[row * picks + p].astype(jnp.float32)
        block = total[:, p * size : (p + 1) * size] - on_diag * eye
        out_ref[row * picks + p] = block.astype(out_ref.dtype)


def store_scores(row, total, unused_ref, out_ref):
    size = total.shape[0]
    out_ref[pl.ds(row, 1), :] = jnp.sum(total * total, axis=0, keepdims=True) / size


def flat_numbers(values):
    return jnp.stack([jnp.asarray(v, jnp.int32) for v in values])


def call_all(a_all, tables, table_size, pick, after, extra, finish, out_shape, out_dtype):
    rows, slots, n_picks = pick.shape
    size = a_all.shape[-1]
    smem = pl.BlockSpec(memory_space=pltpu.SMEM)
    anywhere = pl.BlockSpec(memory_space=pl.ANY)
    vmem = pl.BlockSpec(memory_space=pltpu.VMEM)
    return pl.pallas_call(
        functools.partial(all_slots, [span or (0, t.shape[0]) for t, span, _ in tables], n_picks, finish),
        out_shape=jax.ShapeDtypeStruct(out_shape, out_dtype),
        in_specs=[smem] * 4 + [vmem] + [anywhere] * len(tables),
        out_specs=vmem,
        scratch_shapes=[
            pltpu.VMEM((table_size + 1, size, size), jnp.bfloat16),
            pltpu.SemaphoreType.DMA((len(tables),)),
        ],
        compiler_params=pltpu.CompilerParams(
            vmem_limit_bytes=(table_size + 1) * size * size * 2 + 2**21
        ),
        cost_estimate=pl.CostEstimate(
            flops=10 * rows * slots * n_picks * size**3,
            bytes_accessed=rows * slots * size * size * 6,
            transcendentals=0,
        ),
    )(
        pick.reshape(-1).astype(jnp.int32),
        flat_numbers([start for _, _, start in tables]),
        after,
        extra.reshape(-1).astype(jnp.int32),
        a_all,
        *[table for table, _, _ in tables],
    )


def on_device(acol, aval, mcol, mval, rpat, scol, cand):
    n_rows, n_blk = lax.axis_size("rows"), lax.axis_size("blk")
    rows_here, slots_here = acol.shape
    slabs, _, qm, size, _ = mval.shape
    q, c = rpat.shape[2], cand.shape[2]
    groups = n_blk // slabs
    group_rows = rows_here // groups
    total_rows = rows_here * n_rows
    i, j = lax.axis_index("rows"), lax.axis_index("blk")
    x, t = j // slabs, j % slabs
    own_row = x * group_rows

    def move(value, to):
        route = []
        for a in range(n_rows):
            for b in range(n_blk):
                ra, rx, rt = to(a, b // slabs, b % slabs)
                dest = (ra % n_rows) * n_blk + (rx % groups) * slabs + rt % slabs
                route.append((a * n_blk + b, dest))
        return lax.ppermute(value, ("rows", "blk"), route)

    def near_side(a, bx):
        return a + 1 if bx == 0 else a - 1

    def far_side(a, bx):
        return a - 1 if bx == 0 else a + 1

    m_flat = mval.reshape(-1, size, size)
    m_base = t * rows_here * qm
    block_m = group_rows * qm
    before, here, after = 0, rows_here, 2 * rows_here

    def wanted_by(dx):
        return ((x + dx) % groups) * group_rows

    jobs = [(in_hbm(m_flat), m_base, rows_here * qm, 2 * (1 - x) if groups == 2 else 0)]
    jobs += [(in_hbm(aval), wanted_by(dx), group_rows, 0) for dx in range(1, groups)]
    m_own, *sent, token = call_cut(jobs)
    if groups == 2:
        near = move(m_own, lambda a, bx, bt: (near_side(a, bx), bx, bt))
    a_far = [
        move(part, lambda a, bx, bt, dx=dx: (a, bx + dx, bt))
        for dx, part in enumerate(sent, 1)
    ]
    if groups == 2:
        half = group_rows * 3 // 8 * qm
        third = move(m_own[block_m + half :], lambda a, bx, bt: (far_side(a, bx), bx, bt))
        near_part, token = call_cut([(near, 0, half, 0)], 5 * 10**10)
        relayed = move(near_part, lambda a, bx, bt: (a, bx + 1, bt))
        front, back = (0, block_m), (block_m, block_m)
        m_tables = [
            (m_own, front, (here + (1 - x) * group_rows) * qm),
            (m_own, back, (here + x * group_rows) * qm),
            (near, front, jnp.where(x == 0, before + group_rows, after) * qm),
            (near, back, jnp.where(x == 0, before, after + group_rows) * qm),
            (third, None, jnp.where(x == 0, after, before + group_rows) * qm + half),
            (relayed, None, jnp.where(x == 0, after, before + group_rows) * qm),
        ]
    else:
        m_tables = [
            (m_own, None, here * qm),
            (move(m_own, lambda a, bx, bt: (a + 1, bx, bt)), None, before * qm),
            (move(m_own, lambda a, bx, bt: (a - 1, bx, bt)), None, after * qm),
        ]

    tags = jnp.concatenate([mcol, rpat], axis=2)
    if slabs == 2:
        one_side = move(tags, lambda a, bx, bt: (a + 1 if bt == 0 else a - 1, bx, bt))
    else:
        sides = [move(tags, lambda a, bx, bt, d=d: (a + d, bx, bt)) for d in (1, -1)]
    own_cols = [lax.dynamic_slice_in_dim(acol, own_row, group_rows, 0)] + [
        move(
            lax.dynamic_slice_in_dim(acol, wanted_by(dx), group_rows, 0),
            lambda a, bx, bt, dx=dx: (a, bx + dx, bt),
        )
        for dx in range(1, groups)
    ]

    def from_cores(value):
        return [value] + [
            in_hbm(move(value, lambda a, bx, bt, dt=dt: (a, bx, bt + dt)))
            for dt in range(1, slabs)
        ]

    a_pieces = []
    for piece in [aval] + a_far:
        a_pieces += from_cores(piece)
    a_all = call_join(a_pieces, own_row, group_rows)

    own_cols = jnp.stack(own_cols, axis=1)
    if slabs == 2:
        flat = jnp.concatenate([own_cols.reshape(-1), one_side.reshape(-1)])
        other = move(flat + token, lambda a, bx, bt: (a, bx, bt + 1))
        cols = jnp.stack([own_cols, other[: own_cols.size].reshape(own_cols.shape)], axis=2)
        other_side = other[own_cols.size :].reshape(tags.shape)
        sides = [
            jnp.where(t == 0, one_side, other_side), jnp.where(t == 0, other_side, one_side)
        ]
    else:
        cols = jnp.stack(
            [own_cols]
            + [
                move(own_cols, lambda a, bx, bt, dt=dt: (a, bx, bt + dt))
                for dt in range(1, slabs)
            ],
            axis=2,
        )
    cols = cols.reshape(group_rows, -1)
    tags_ext = jnp.concatenate([sides[0], tags, sides[1]], axis=1)
    tags_ext = lax.dynamic_index_in_dim(tags_ext, t, 0, keepdims=False)
    present = cols >= 0
    position = jnp.where(present, (cols - i * rows_here + rows_here) % total_rows, 0)
    at_row = position[:, :, None] == jnp.arange(3 * rows_here)[None, None, :]
    near_tags = jnp.sum(jnp.where(at_row[:, :, :, None], tags_ext[None, None], 0), axis=2)
    pattern = lax.dynamic_slice(rpat, (t, own_row, 0), (1, group_rows, q))[0]
    wanted = lax.dynamic_slice(cand, (t, own_row, 0), (1, group_rows, c))[0]

    def picks(near, targets):
        width = near.shape[2]
        empty = 3 * rows_here * width
        hit = (near[:, :, :, None] == targets[:, None, None, :]) & present[:, :, None, None]
        at = position[:, :, None, None] * width + jnp.arange(width)[None, None, :, None]
        return empty + jnp.sum(jnp.where(hit, at - empty, 0), axis=2)

    m_pick = picks(near_tags[:, :, :qm], pattern)
    r_pick = picks(near_tags[:, :, qm:], wanted)
    slab_range = jnp.arange(scol.shape[1], dtype=jnp.int32)
    owner_row = lax.dynamic_index_in_dim(scol, t, 0, keepdims=False)
    owners = jnp.sum(
        jnp.where(pattern[:, :, None] == slab_range, owner_row[None, None, :], 0), axis=2
    )
    local_ids = i * rows_here + own_row + jnp.arange(group_rows, dtype=jnp.int32)
    on_diag = (owners == local_ids[:, None]).astype(jnp.int32)

    resid = call_all(
        a_all, m_tables, 3 * rows_here * qm, m_pick, jnp.zeros(1, jnp.int32), on_diag, store_residual,
        (group_rows * q, size, size), jnp.bfloat16,
    )

    block_r = group_rows * q
    if groups == 2:
        r_far = move(resid, lambda a, bx, bt: (far_side(a, bx), bx, bt))
        r_peer = move(resid, lambda a, bx, bt: (a, bx + 1, bt))
        r_next, r_far = lax.optimization_barrier((resid, r_far))
        r_near = move(r_next, lambda a, bx, bt: (near_side(a, bx), bx, bt))
        r_relay = move(r_far, lambda a, bx, bt: (a, bx + 1, bt))
        parts = [r_next, r_peer]
        r_tables = [
            (r_next, None, (here + own_row) * q),
            (r_peer, None, (here + (1 - x) * group_rows) * q),
            (r_near, None, jnp.where(x == 0, before, after + group_rows) * q),
            (r_far, None, jnp.where(x == 0, after, before + group_rows) * q),
            (r_relay, None, jnp.where(x == 0, before + group_rows, after) * q),
        ]
    else:
        parts = [resid]
        for dx in range(1, groups):
            parts.append(move(resid, lambda a, bx, bt, dx=dx: (a, bx + dx, bt)))
        order = (x - jnp.arange(groups)) % groups
        r_here = jnp.take(jnp.stack(parts), order, axis=0).reshape(-1, size, size)
        r_tables = [
            (r_here, None, here * q),
            (move(r_here, lambda a, bx, bt: (a + 1, bx, bt)), None, before * q),
            (move(r_here, lambda a, bx, bt: (a - 1, bx, bt)), None, after * q),
        ]

    width = size // n_blk
    shared = []
    for dx, part in enumerate(parts):
        for dt, moved in enumerate(from_cores(part)):
            shared.append((moved, (t - dt) % slabs, ((x - dx) % groups) * group_rows))
    resid_out, done = call_share(shared, j * width, (slabs, rows_here, q, width, size))
    a_all = call_join(a_pieces, own_row + done[0], group_rows)
    scores = call_all(
        a_all, r_tables, 3 * rows_here * q, r_pick, done, on_diag, store_scores,
        (group_rows, c * size), jnp.float32,
    )
    gathered = lax.all_gather(scores.reshape(group_rows, c, size), "blk")
    gathered = lax.dynamic_slice_in_dim(gathered, j * width, width, 3)
    gathered = gathered.reshape(groups, slabs, group_rows, c, width)
    score_out = jnp.swapaxes(gathered, 0, 1).reshape(slabs, rows_here, c, width)
    return jnp.swapaxes(resid_out, 3, 4), score_out


def solution(mesh):
    placed = (
        P("rows", "blk"),
        P("rows", "blk", None, None),
        P(None, "rows", None),
        P(None, "rows", None, None, None),
        P(None, "rows", None),
        P(),
        P(None, "rows", None),
    )
    return jax.shard_map(
        on_device,
        mesh=mesh,
        in_specs=placed,
        out_specs=(P(None, "rows", None, None, "blk"), P(None, "rows", None, "blk")),
        check_vma=False,
    )
```

time: 134 us -> 128 us (0.955)
  waiting for transfers between devices: 70.4 us -> 64.7 us
  Pallas kernels: 24.3 us -> 28.2 us
  local copies, waits for them, and re-layouts: 10 us -> 6.67 us
  starting transfers between devices: 22.2 us -> 19 us
  other arithmetic: 0.88 us -> 2.4 us
    pallas_call x3 -> x5, Pallas kernels: 15.1 us -> 21.2 us  [the longest x2 12.3 us: call_all(): pl.pallas_call(functools.partial(all_slots, [span or (0, t.shape[0]) for...]
    ppermute x15, waiting for transfers between devices: 70.4 us -> 64.7 us  [move(): return lax.ppermute(value, ('rows', 'blk'), route)]
    unnamed x30 -> x21, local copies, waits for them, and re-layouts: 6.64 us -> 2.73 us
    ppermute x15, starting transfers between devices: 22.2 us -> 19 us  [move(): return lax.ppermute(value, ('rows', 'blk'), route)]
    pallas_call x3 -> x2, Pallas kernels: 9.19 us -> 6.93 us  [call_cut(): pl.pallas_call(functools.partial(cut_rows, counts, pieces), out_shape=[pl...]
    slice x0 -> x1, local copies, waits for them, and re-layouts: none -> 2 us  [on_device(): m_own[block_m + half:]]
  transfers between devices with their start and end apart: 15 -> 15, of which waited for: 8 -> 8; matrix products, arithmetic and copies ran while one was open for 4% -> 5% of each run, Pallas kernels for 5% -> 9%
where the time goes in v1:
time: 128 us
  waiting for transfers between devices  64.7 us (51%)
  Pallas kernels  28.2 us (22%)
  starting transfers between devices  19 us (15%)
  local copies, waits for them, and re-layouts  6.67 us (5%)
  blocking collectives  5.19 us (4%)
  other arithmetic  2.4 us (2%)
  between operations  1.67 us (1%)
    ppermute x15, waiting for transfers between devices, move(): return lax.ppermute(value, ('rows', 'blk'), route)  64.7 us
    ppermute x15, starting transfers between devices, move(): return lax.ppermute(value, ('rows', 'blk'), route)  19 us
    pallas_call x2, Pallas kernels, call_all(): pl.pallas_call(functools.partial(all_slots, [span or (0, t.shape[0]) for...  12.3 us
    pallas_call x2, Pallas kernels, call_cut(): pl.pallas_call(functools.partial(cut_rows, counts, pieces), out_shape=[pl...  6.93 us
    pallas_call x2, Pallas kernels, call_join(): pl.pallas_call(functools.partial(join_pieces, len(pieces)), out_shape=plt...  5.98 us
    all_gather x1, blocking collectives, on_device(): gathered = lax.all_gather(scores.reshape(group_rows, c, size), 'blk')  5.19 us
    pallas_call x1, Pallas kernels, call_share(): pl.pallas_call(functools.partial(share_columns, len(parts)), out_shape=[j...  3 us
    unnamed x21, local copies, waits for them, and re-layouts  2.73 us
  transfers between devices with their start and end apart: 15, of which 8 were waited for; matrix products, arithmetic and copies ran while one was open for 5% of the time, Pallas kernels for 9%

profile of v1, /device:TPU:0, one launch (start us, length us, event | category | flops | bytes accessed | tf_op | source)
XLA Modules:
  0.0 127.7 jit_solution(478515020340779381)
XLA Ops:
  0.6 0.0 copy-start
  0.7 0.1 pad_add_fusion.5
  0.8 4.7 %shard_map.86 = (bf16[64,128,128]{2,1,0:T(8,128)(2,1)}, bf16[8,8,128,128]{3,2,1,0:T(8,128)(2,1)}, s32[1]{0:T(128)}) custom-call(s32[2]{0:T(128)S(1)} %get-tuple-element.36.start_ref, s32[2]{0:T(128)S(1)} %get-tuple-element.37.turn_ref, bf16[128,128,128]{2,1,0:T(8,128)(2,1)} %bitcast.45, bf16[16,8,128,128]{3,2,1,0:T(8,128)(2,1)} %refs_0_.3), custom_call_target="tpu_custom_call" | custom-call | flops 1000000000 | bytes 4194304 | tf_op jit(solution)/shard_map/pallas_call | solution.py:130
  5.4 3.0 %collective-permute-start.5 = (bf16[8,8,128,128]{3,2,1,0:T(8,128)(2,1)}, bf16[8,8,128,128]{3,2,1,0:T(8,128)(2,1)S(1)}, u32[]{:S(2)}, u32[]{:S(2)}) collective-permute-start(bf16[8,8,128,128]{3,2,1,0:T(8,128)(2,1)} %get-tuple-element.12), channel_id=1, source_target_pairs={{0,2},{1,3},{2,0},{3,1},{4,6},{5,7},{6,4},{7,5},{8,10},{9,11},{10,... | collective-permute-start | bytes 6291464 | tf_op jit(solution)/shard_map/ppermute | solution.py:262
  8.5 1.5 %collective-permute-start.2 = (bf16[64,128,128]{2,1,0:T(8,128)(2,1)}, bf16[64,128,128]{2,1,0:T(8,128)(2,1)}, u32[]{:S(2)}, u32[]{:S(2)}) collective-permute-start(bf16[64,128,128]{2,1,0:T(8,128)(2,1)} %get-tuple-element.10.refs_0_.refs_1_), channel_id=1, source_target_pairs={{0,4},{1,5},{2,30},{3,31},{4,8},{5,9},{6,2},{7,3},{8,12},{9,13},{1... | collective-permute-start | bytes 6291464 | tf_op jit(solution)/shard_map/ppermute | solution.py:262
  10.0 0.1 constant_dynamic-slice_fusion.5
  10.1 0.1 copy.130
  10.1 3.6 %collective-permute-start = (s32[8,8]{1,0:T(8,128)S(1)}, s32[8,8]{1,0:T(8,128)S(1)}, u32[]{:S(2)}, u32[]{:S(2)}) collective-permute-start(s32[8,8]{1,0:T(8,128)S(1)} %copy.130), channel_id=1, source_target_pairs={{0,2},{1,3},{2,0},{3,1},{4,6},{5,7},{6,4},{7,5},{8,10},{9,11},{10,... | collective-permute-start | bytes 776 | tf_op jit(solution)/shard_map/ppermute | solution.py:262
  13.7 0.1 copy.113
  13.8 0.1 copy.114
  13.9 0.1 pad_add_fusion
  14.0 0.1 fusion.6
  14.1 0.2 select_reduce_fusion.3
  14.3 2.0 %slice.26 = bf16[20,128,128]{2,1,0:T(8,128)(2,1)} slice(bf16[64,128,128]{2,1,0:T(8,128)(2,1)} %get-tuple-element.10.refs_0_.refs_1_), slice={[44:64], [0:128], [0:128]} | slice | bytes 1310720 | tf_op jit(solution)/shard_map/slice | solution.py:289
  16.3 0.1 copy.129
  16.4 38.0 %collective-permute-done = s32[8,8]{1,0:T(8,128)S(1)} collective-permute-done((s32[8,8]{1,0:T(8,128)S(1)}, s32[8,8]{1,0:T(8,128)S(1)}, u32[]{:S(2)}, u32[]{:S(2)}) %collective-permute-start) | collective-permute-done | bytes 288 | tf_op jit(solution)/shard_map/ppermute | solution.py:262
  54.4 4.8 %collective-permute-start.7 = (bf16[20,128,128]{2,1,0:T(8,128)(2,1)}, bf16[20,128,128]{2,1,0:T(8,128)(2,1)S(1)}, u32[]{:S(2)}, u32[]{:S(2)}) collective-permute-start(bf16[20,128,128]{2,1,0:T(8,128)(2,1)} %slice.26), channel_id=1, source_target_pairs={{0,28},{1,29},{2,6},{3,7},{4,0},{5,1},{6,10},{7,11},{8,4},{9,5},{1... | collective-permute-start | bytes 1966088 | tf_op jit(solution)/shard_map/ppermute | solution.py:262
  59.2 0.1 reshape.152
  59.3 0.1 reshape.153
  59.4 0.1 collective-permute-start.6
  59.5 2.3 %shard_map.87 = (bf16[12,128,128]{2,1,0:T(8,128)(2,1)}, s32[1]{0:T(128)}) custom-call(s32[1]{0:T(128)} %constant.108.clone.1.start_ref.turn_ref.after_ref, s32[1]{0:T(128)} %constant.108.clone.1.start_ref.turn_ref.after_ref, bf16[64,128,128]{2,1,0:T(8,128)(2,1)} %collective-permute-done.2.refs_0_.refs_2_.refs_3_), custom_call_target="tpu_custom_call" | custom-call | flops 49999998976 | bytes 4194304 | tf_op jit(solution)/shard_map/pallas_call | solution.py:130
  61.8 0.7 add_add_fusion.2
  62.5 0.5 collective-permute-start.3
  63.0 0.1 copy.123
  63.1 0.1 reshape.160.extra_ref
  63.2 0.1 stack.113.start_ref
  63.2 0.0 collective-permute-start.8
  63.3 0.6 collective-permute-done.3
  63.8 0.1 stack_reshape.3
  64.0 0.1 add.204
  64.1 0.1 copy.116
  64.1 0.1 copy.118
  64.2 0.1 reshape.155
  64.4 0.1 fusion.1
  64.4 0.1 copy.119
  64.5 0.1 iota_compare_fusion
  64.6 0.9 select_reduce_fusion
  65.6 0.1 select_reduce_fusion.1
  65.7 0.1 copy.122
  65.8 0.1 add.212.pick_ref
  66.0 3.0 %shard_map.88.a_ref = bf16[8,32,128,128]{3,2,1,0:T(8,128)(2,1)S(1)} custom-call(s32[1]{0:T(128)} %bitcast.23.first_ref, bf16[16,8,128,128]{3,2,1,0:T(8,128)(2,1)} %refs_0_.3, bf16[16,8,128,128]{3,2,1,0:T(8,128)(2,1)} %collective-permute-done.4.refs_1_, bf16[8,8,128,128]{3,2,1,0:T(8,128)(2,1)S(1)} %collective-permute-done.5.refs_2_, ...), custom_call_target="tpu_custom_call" | custom-call | flops 1000000000 | bytes 16777216 | tf_op jit(solution)/shard_map/pallas_call | solution.py:80
  69.0 3.9 %collective-permute-done.7.refs_4_ = bf16[20,128,128]{2,1,0:T(8,128)(2,1)S(1)} collective-permute-done((bf16[20,128,128]{2,1,0:T(8,128)(2,1)}, bf16[20,128,128]{2,1,0:T(8,128)(2,1)S(1)}, u32[]{:S(2)}, u32[]{:S(2)}) %collective-permute-start.7) | collective-permute-done | bytes 655392 | tf_op jit(solution)/shard_map/ppermute | solution.py:262
  72.9 1.6 %collective-permute-done.8.refs_5_ = bf16[12,128,128]{2,1,0:T(8,128)(2,1)S(1)} collective-permute-done((bf16[12,128,128]{2,1,0:T(8,128)(2,1)}, bf16[12,128,128]{2,1,0:T(8,128)(2,1)S(1)}, u32[]{:S(2)}, u32[]{:S(2)}) %collective-permute-start.8) | collective-permute-done | bytes 393248 | tf_op jit(solution)/shard_map/ppermute | solution.py:262
  74.5 0.7 copy-done.2
  75.3 1.0 copy-done.3
  76.3 5.9 %shard_map.89.refs_0_ = bf16[16,128,128]{2,1,0:T(8,128)(2,1)S(1)} custom-call(s32[512]{0:T(512)S(1)} %add.212.pick_ref, s32[6]{0:T(128)S(1)} %stack.113.start_ref, s32[1]{0:T(128)} %constant.108.clone.1.start_ref.turn_ref.after_ref, s32[16]{0:T(128)S(1)} %reshape.160.extra_ref, bf16[8,32,128,128]{3,2,1,0:T(8,128)(2,1)S(1)} %shard_map.88.a_ref, ...), custom_call_target="tpu_custom_call" | custom-call | flops 10737418240 | bytes 25165824 | tf_op jit(solution)/shard_map/pallas_call | solution.py:216
  82.2 3.3 %collective-permute-start.9 = (bf16[16,128,128]{2,1,0:T(8,128)(2,1)S(1)}, bf16[16,128,128]{2,1,0:T(8,128)(2,1)S(1)}, u32[]{:S(2)}, u32[]{:S(2)}) collective-permute-start(bf16[16,128,128]{2,1,0:T(8,128)(2,1)S(1)} %shard_map.89.refs_0_), channel_id=1, source_target_pairs={{0,28},{1,29},{2,6},{3,7},{4,0},{5,1},{6,10},{7,11},{8,4},{9,5},{1... | collective-permute-start | bytes 1572872 | tf_op jit(solution)/shard_map/ppermute | solution.py:262
  85.5 0.1 stack.119.start_ref
  85.6 0.1 fusion.7
  85.7 0.1 pad_add_fusion.3
  85.8 10.2 %collective-permute-done.9.refs_3_ = bf16[16,128,128]{2,1,0:T(8,128)(2,1)S(1)} collective-permute-done((bf16[16,128,128]{2,1,0:T(8,128)(2,1)S(1)}, bf16[16,128,128]{2,1,0:T(8,128)(2,1)S(1)}, u32[]{:S(2)}, u32[]{:S(2)}) %collective-permute-start.9) | collective-permute-done | bytes 524320 | tf_op jit(solution)/shard_map/ppermute | solution.py:262
  96.0 2.3 %collective-permute-done.11.refs_2_.refs_1_ = bf16[16,128,128]{2,1,0:T(8,128)(2,1)} collective-permute-done((bf16[16,128,128]{2,1,0:T(8,128)(2,1)S(1)}, bf16[16,128,128]{2,1,0:T(8,128)(2,1)}, u32[]{:S(2)}, u32[]{:S(2)}) %collective-permute-start.11) | collective-permute-done | bytes 524320 | tf_op jit(solution)/shard_map/ppermute | solution.py:262
  98.3 2.1 %collective-permute-start.14 = (bf16[16,128,128]{2,1,0:T(8,128)(2,1)S(1)}, bf16[16,128,128]{2,1,0:T(8,128)(2,1)}, u32[]{:S(2)}, u32[]{:S(2)}) collective-permute-start(bf16[16,128,128]{2,1,0:T(8,128)(2,1)S(1)} %collective-permute-done.9.refs_3_), channel_id=1, source_target_pairs={{0,2},{1,3},{2,0},{3,1},{4,6},{5,7},{6,4},{7,5},{8,10},{9,11},{10,... | collective-permute-start | bytes 1572872 | tf_op jit(solution)/shard_map/ppermute | solution.py:262
  100.4 0.1 select_reduce_fusion.2
  100.5 0.1 copy.126
  100.7 0.1 add.223.pick_ref
  100.8 3.0 %shard_map.90 = (bf16[2,16,2,32,128]{4,3,2,1,0:T(8,128)(2,1)}, s32[1]{0:T(128)}) custom-call(s32[1]{0:T(128)} %bitcast.column_ref, s32[4]{0:T(128)S(1)} %get-tuple-element.34.slab_ref, s32[4]{0:T(128)S(1)} %get-tuple-element.35.first_ref, bf16[16,128,128]{2,1,0:T(8,128)(2,1)S(1)} %shard_map.89.refs_0_, ...), custom_call_target="tpu_custom_call" | custom-call | flops 1000000000 | bytes 4194304 | tf_op jit(solution)/shard_map/pallas_call | solution.py:173
  104.5 2.9 %shard_map.91.a_ref = bf16[8,32,128,128]{3,2,1,0:T(8,128)(2,1)S(1)} custom-call(s32[1]{0:T(128)} %bitcast.32.first_ref, bf16[16,8,128,128]{3,2,1,0:T(8,128)(2,1)} %refs_0_.3, bf16[16,8,128,128]{3,2,1,0:T(8,128)(2,1)} %collective-permute-done.4.refs_1_, bf16[8,8,128,128]{3,2,1,0:T(8,128)(2,1)S(1)} %collective-permute-done.5.refs_2_, ...), custom_call_target="tpu_custom_call" | custom-call | flops 1000000000 | bytes 16777216 | tf_op jit(solution)/shard_map/pallas_call | solution.py:80
  107.4 5.4 %collective-permute-done.14.refs_4_ = bf16[16,128,128]{2,1,0:T(8,128)(2,1)} collective-permute-done((bf16[16,128,128]{2,1,0:T(8,128)(2,1)S(1)}, bf16[16,128,128]{2,1,0:T(8,128)(2,1)}, u32[]{:S(2)}, u32[]{:S(2)}) %collective-permute-start.14) | collective-permute-done | bytes 524320 | tf_op jit(solution)/shard_map/ppermute | solution.py:262
  112.8 2.6 %collective-permute-done.13.refs_2_ = bf16[16,128,128]{2,1,0:T(8,128)(2,1)} collective-permute-done((bf16[16,128,128]{2,1,0:T(8,128)(2,1)S(1)}, bf16[16,128,128]{2,1,0:T(8,128)(2,1)}, u32[]{:S(2)}, u32[]{:S(2)}) %collective-permute-start.13) | collective-permute-done | bytes 524320 | tf_op jit(solution)/shard_map/ppermute | solution.py:262
  115.5 6.3 %shard_map.92 = f32[8,256]{1,0:T(8,128)S(1)} custom-call(s32[512]{0:T(512)S(1)} %add.223.pick_ref, s32[5]{0:T(128)S(1)} %stack.119.start_ref, s32[1]{0:T(128)} %get-tuple-element.16.after_ref, s32[16]{0:T(128)S(1)} %reshape.160.extra_ref, bf16[8,32,128,128]{3,2,1,0:T(8,128)(2,1)S(1)} %shard_map.91.a_ref, bf16[16,128,128]{2,1,0:T(8,128)(2,1)S(1)} %shard_map.89.refs_0_, ...), custom_call_target="tpu_custom_call" | custom-call | flops 10737418240 | bytes 25165824 | tf_op jit(solution)/shard_map/pallas_call | solution.py:216
  121.8 5.2 %all_gather.3 = f32[4,8,2,128]{3,1,2,0:T(8,128)S(1)} all-gather(f32[1,8,2,128]{3,1,2,0:T(8,128)S(1)} %bitcast.44), channel_id=1, replica_groups=mesh['rows'=8,'blk'=4] {'blk'}, dimensions={0}, use_global_device_ids=true | all-gather | bytes 40960 | tf_op jit(solution)/shard_map/all_gather | solution.py:420
  127.0 0.1 constant_dynamic-slice_fusion
  127.1 0.6 copy.128
  (49 shorter events, 0.2 us)
Async XLA Ops:
  0.6 85.0 %copy-start = (s32[2,16,2]{1,2,0:T(2,128)S(1)}, s32[2,16,2]{1,2,0:T(2,128)}, u32[]{:S(2)}) copy-start(s32[2,16,2]{1,2,0:T(2,128)} %param.13) | copy-start | bytes 772
  0.8 9.2 %copy-start.4 = (s32[16,8]{0,1:T(8,128)S(1)}, s32[16,8]{0,1:T(8,128)}, u32[]{:S(2)}) copy-start(s32[16,8]{0,1:T(8,128)} %param.7) | copy-start | bytes 1540
  0.8 12.9 %copy-start.6 = (s32[2,16,4]{1,2,0:T(4,128)S(1)}, s32[2,16,4]{1,2,0:T(4,128)}, u32[]{:S(2)}) copy-start(s32[2,16,4]{1,2,0:T(4,128)} %param.9) | copy-start | bytes 1540
  0.8 13.0 %copy-start.5 = (s32[2,16,2]{1,2,0:T(2,128)S(1)}, s32[2,16,2]{1,2,0:T(2,128)}, u32[]{:S(2)}) copy-start(s32[2,16,2]{1,2,0:T(2,128)} %param.11) | copy-start | bytes 772
  0.8 13.2 %copy-start.7 = (s32[2,64]{1,0:T(2,128)S(1)}, s32[2,64]{1,0:T(2,128)}, u32[]{:S(2)}) copy-start(s32[2,64]{1,0:T(2,128)} %param.12) | copy-start | bytes 1540
  5.4 54.0 %collective-permute-start.5 = (bf16[8,8,128,128]{3,2,1,0:T(8,128)(2,1)}, bf16[8,8,128,128]{3,2,1,0:T(8,128)(2,1)S(1)}, u32[]{:S(2)}, u32[]{:S(2)}) collective-permute-start(bf16[8,8,128,128]{3,2,1,0:T(8,128)(2,1)} %get-tuple-element.12), channel_id=1, source_target_pairs={{0,2},{1,3},{2,0},{3,1},{4,6},{5,7},{6,4},{7,5},{8,10},{9,11},{10,... | collective-permute-start | bytes 6291464 | tf_op jit(solution)/shard_map/ppermute | solution.py:262
  8.5 51.1 %collective-permute-start.2 = (bf16[64,128,128]{2,1,0:T(8,128)(2,1)}, bf16[64,128,128]{2,1,0:T(8,128)(2,1)}, u32[]{:S(2)}, u32[]{:S(2)}) collective-permute-start(bf16[64,128,128]{2,1,0:T(8,128)(2,1)} %get-tuple-element.10.refs_0_.refs_1_), channel_id=1, source_target_pairs={{0,4},{1,5},{2,30},{3,31},{4,8},{5,9},{6,2},{7,3},{8,12},{9,13},{1... | collective-permute-start | bytes 6291464 | tf_op jit(solution)/shard_map/ppermute | solution.py:262
  10.0 56.0 %collective-permute-start.4 = (bf16[16,8,128,128]{3,2,1,0:T(8,128)(2,1)}, bf16[16,8,128,128]{3,2,1,0:T(8,128)(2,1)}, u32[]{:S(2)}, u32[]{:S(2)}) collective-permute-start(bf16[16,8,128,128]{3,2,1,0:T(8,128)(2,1)} %refs_0_.3), channel_id=1, source_target_pairs={{0,1},{1,0},{2,3},{3,2},{4,5},{5,4},{6,7},{7,6},{8,9},{9,8},{10,11... | collective-permute-start | bytes 12582920 | tf_op jit(solution)/shard_map/ppermute | solution.py:262
  10.1 44.3 %collective-permute-start = (s32[8,8]{1,0:T(8,128)S(1)}, s32[8,8]{1,0:T(8,128)S(1)}, u32[]{:S(2)}, u32[]{:S(2)}) collective-permute-start(s32[8,8]{1,0:T(8,128)S(1)} %copy.130), channel_id=1, source_target_pairs={{0,2},{1,3},{2,0},{3,1},{4,6},{5,7},{6,4},{7,5},{8,10},{9,11},{10,... | collective-permute-start | bytes 776 | tf_op jit(solution)/shard_map/ppermute | solution.py:262
  14.0 45.3 %collective-permute-start.1 = (s32[2,16,6]{2,1,0:T(8,128)S(1)}, s32[2,16,6]{2,1,0:T(8,128)S(1)}, u32[]{:S(2)}, u32[]{:S(2)}) collective-permute-start(s32[2,16,6]{2,1,0:T(8,128)S(1)} %pad_add_fusion), channel_id=1, source_target_pairs={{0,4},{1,29},{2,6},{3,31},{4,8},{5,1},{6,10},{7,3},{8,12},{9,5},{1... | collective-permute-start | bytes 2312 | tf_op jit(solution)/shard_map/ppermute | solution.py:262
  54.4 18.5 %collective-permute-start.7 = (bf16[20,128,128]{2,1,0:T(8,128)(2,1)}, bf16[20,128,128]{2,1,0:T(8,128)(2,1)S(1)}, u32[]{:S(2)}, u32[]{:S(2)}) collective-permute-start(bf16[20,128,128]{2,1,0:T(8,128)(2,1)} %slice.26), channel_id=1, source_target_pairs={{0,28},{1,29},{2,6},{3,7},{4,0},{5,1},{6,10},{7,11},{8,4},{9,5},{1... | collective-permute-start | bytes 1966088 | tf_op jit(solution)/shard_map/ppermute | solution.py:262
  59.4 6.5 %collective-permute-start.6 = (bf16[8,8,128,128]{3,2,1,0:T(8,128)(2,1)S(1)}, bf16[8,8,128,128]{3,2,1,0:T(8,128)(2,1)}, u32[]{:S(2)}, u32[]{:S(2)}) collective-permute-start(bf16[8,8,128,128]{3,2,1,0:T(8,128)(2,1)S(1)} %collective-permute-done.5.refs_2_), channel_id=1, source_target_pairs={{0,1},{1,0},{2,3},{3,2},{4,5},{5,4},{6,7},{7,6},{8,9},{9,8},{10,11... | collective-permute-start | bytes 6291464 | tf_op jit(solution)/shard_map/ppermute | solution.py:262
  62.5 1.4 %collective-permute-start.3 = (s32[320]{0:T(512)S(1)}, s32[320]{0:T(512)S(1)}, u32[]{:S(2)}, u32[]{:S(2)}) collective-permute-start(s32[320]{0:T(512)S(1)} %add_add_fusion.2), channel_id=1, source_target_pairs={{0,1},{1,0},{2,3},{3,2},{4,5},{5,4},{6,7},{7,6},{8,9},{9,8},{10,11... | collective-permute-start | bytes 3848 | tf_op jit(solution)/shard_map/ppermute | solution.py:262
  63.2 11.3 %collective-permute-start.8 = (bf16[12,128,128]{2,1,0:T(8,128)(2,1)}, bf16[12,128,128]{2,1,0:T(8,128)(2,1)S(1)}, u32[]{:S(2)}, u32[]{:S(2)}) collective-permute-start(bf16[12,128,128]{2,1,0:T(8,128)(2,1)} %get-tuple-element.13), channel_id=1, source_target_pairs={{0,2},{1,3},{2,0},{3,1},{4,6},{5,7},{6,4},{7,5},{8,10},{9,11},{10,... | collective-permute-start | bytes 1179656 | tf_op jit(solution)/shard_map/ppermute | solution.py:262
  66.0 9.3 %copy-start.1 = (bf16[64,128,128]{2,1,0:T(8,128)(2,1)S(1)}, bf16[64,128,128]{2,1,0:T(8,128)(2,1)}, u32[]{:S(2)}) copy-start(bf16[64,128,128]{2,1,0:T(8,128)(2,1)} %get-tuple-element.10.refs_0_.refs_1_) | copy-start | bytes 6291460
  74.5 0.7 copy-start.2
  75.3 1.0 copy-start.3
  82.2 13.8 %collective-permute-start.9 = (bf16[16,128,128]{2,1,0:T(8,128)(2,1)S(1)}, bf16[16,128,128]{2,1,0:T(8,128)(2,1)S(1)}, u32[]{:S(2)}, u32[]{:S(2)}) collective-permute-start(bf16[16,128,128]{2,1,0:T(8,128)(2,1)S(1)} %shard_map.89.refs_0_), channel_id=1, source_target_pairs={{0,28},{1,29},{2,6},{3,7},{4,0},{5,1},{6,10},{7,11},{8,4},{9,5},{1... | collective-permute-start | bytes 1572872 | tf_op jit(solution)/shard_map/ppermute | solution.py:262
  85.5 12.8 %collective-permute-start.11 = (bf16[16,128,128]{2,1,0:T(8,128)(2,1)S(1)}, bf16[16,128,128]{2,1,0:T(8,128)(2,1)}, u32[]{:S(2)}, u32[]{:S(2)}) collective-permute-start(bf16[16,128,128]{2,1,0:T(8,128)(2,1)S(1)} %shard_map.89.refs_0_), channel_id=1, source_target_pairs={{0,2},{1,3},{2,0},{3,1},{4,6},{5,7},{6,4},{7,5},{8,10},{9,11},{10,... | collective-permute-start | bytes 1572872 | tf_op jit(solution)/shard_map/ppermute | solution.py:262
  96.0 4.8 %collective-permute-start.10 = (bf16[16,128,128]{2,1,0:T(8,128)(2,1)S(1)}, bf16[16,128,128]{2,1,0:T(8,128)(2,1)}, u32[]{:S(2)}, u32[]{:S(2)}) collective-permute-start(bf16[16,128,128]{2,1,0:T(8,128)(2,1)S(1)} %shard_map.89.refs_0_), channel_id=1, source_target_pairs={{0,1},{1,0},{2,3},{3,2},{4,5},{5,4},{6,7},{7,6},{8,9},{9,8},{10,11... | collective-permute-start | bytes 1572872 | tf_op jit(solution)/shard_map/ppermute | solution.py:262
  98.3 2.5 %collective-permute-start.12 = (bf16[16,128,128]{2,1,0:T(8,128)(2,1)}, bf16[16,128,128]{2,1,0:T(8,128)(2,1)}, u32[]{:S(2)}, u32[]{:S(2)}) collective-permute-start(bf16[16,128,128]{2,1,0:T(8,128)(2,1)} %collective-permute-done.11.refs_2_.refs_1_), channel_id=1, source_target_pairs={{0,1},{1,0},{2,3},{3,2},{4,5},{5,4},{6,7},{7,6},{8,9},{9,8},{10,11... | collective-permute-start | bytes 1572872 | tf_op jit(solution)/shard_map/ppermute | solution.py:262
  98.3 17.1 %collective-permute-start.13 = (bf16[16,128,128]{2,1,0:T(8,128)(2,1)S(1)}, bf16[16,128,128]{2,1,0:T(8,128)(2,1)}, u32[]{:S(2)}, u32[]{:S(2)}) collective-permute-start(bf16[16,128,128]{2,1,0:T(8,128)(2,1)S(1)} %shard_map.89.refs_0_), channel_id=1, source_target_pairs={{0,4},{1,5},{2,30},{3,31},{4,8},{5,9},{6,2},{7,3},{8,12},{9,13},{1... | collective-permute-start | bytes 1572872 | tf_op jit(solution)/shard_map/ppermute | solution.py:262
  98.3 14.5 %collective-permute-start.14 = (bf16[16,128,128]{2,1,0:T(8,128)(2,1)S(1)}, bf16[16,128,128]{2,1,0:T(8,128)(2,1)}, u32[]{:S(2)}, u32[]{:S(2)}) collective-permute-start(bf16[16,128,128]{2,1,0:T(8,128)(2,1)S(1)} %collective-permute-done.9.refs_3_), channel_id=1, source_target_pairs={{0,2},{1,3},{2,0},{3,1},{4,6},{5,7},{6,4},{7,5},{8,10},{9,11},{10,... | collective-permute-start | bytes 1572872 | tf_op jit(solution)/shard_map/ppermute | solution.py:262

commit v2 on v1

--- a/solution.py
+++ b/solution.py
@@ -287,7 +287,7 @@
     if groups == 2:
         half = group_rows * 3 // 8 * qm
         third = move(m_own[block_m + half :], lambda a, bx, bt: (far_side(a, bx), bx, bt))
-        near_part, token = call_cut([(near, 0, half, 0)], 5 * 10**10)
+        near_part, token = call_cut([(near, 0, half, 0)], 2 * 10**11)
         relayed = move(near_part, lambda a, bx, bt: (a, bx + 1, bt))
         front, back = (0, block_m), (block_m, block_m)
         m_tables = [

time: 128 us -> 125 us (0.977)
  waiting for transfers between devices: 64.7 us -> 61.1 us
  other arithmetic: 2.4 us -> 4.21 us
    ppermute x15, waiting for transfers between devices: 64.7 us -> 61.1 us  [move(): return lax.ppermute(value, ('rows', 'blk'), route)]
    unnamed x21 -> x37, local copies, waits for them, and re-layouts: 2.73 us -> 1.03 us
  transfers between devices with their start and end apart: 15 -> 15, of which waited for: 8 -> 8; matrix products, arithmetic and copies ran while one was open for 5% -> 8% of each run, Pallas kernels for 9% -> 9%
where the time goes in v2:
time: 125 us
  waiting for transfers between devices  61.1 us (49%)
  Pallas kernels  27.7 us (22%)
  starting transfers between devices  18.8 us (15%)
  local copies, waits for them, and re-layouts  6.06 us (5%)
  blocking collectives  5.19 us (4%)
  other arithmetic  4.21 us (3%)
  between operations  1.8 us (1%)
    ppermute x15, waiting for transfers between devices, move(): return lax.ppermute(value, ('rows', 'blk'), route)  61.1 us
    ppermute x15, starting transfers between devices, move(): return lax.ppermute(value, ('rows', 'blk'), route)  18.8 us
    pallas_call x2, Pallas kernels, call_all(): pl.pallas_call(functools.partial(all_slots, [span or (0, t.shape[0]) for...  11.2 us
    pallas_call x2, Pallas kernels, call_join(): pl.pallas_call(functools.partial(join_pieces, len(pieces)), out_shape=plt...  7.15 us
    pallas_call x2, Pallas kernels, call_cut(): pl.pallas_call(functools.partial(cut_rows, counts, pieces), out_shape=[pl...  6.58 us
    all_gather x1, blocking collectives, on_device(): gathered = lax.all_gather(scores.reshape(group_rows, c, size), 'blk')  5.19 us
    pallas_call x1, Pallas kernels, call_share(): pl.pallas_call(functools.partial(share_columns, len(parts)), out_shape=[j...  2.84 us
  transfers between devices with their start and end apart: 15, of which 8 were waited for; matrix products, arithmetic and copies ran while one was open for 8% of the time, Pallas kernels for 9%

profile of v2, /device:TPU:0, one launch (start us, length us, event | category | flops | bytes accessed | tf_op | source)
XLA Modules:
  0.0 125.0 jit_solution(13405284551731005823)
XLA Ops:
  0.6 0.0 copy-start
  0.7 0.1 pad_add_fusion.5
  0.8 4.7 %shard_map.86 = (bf16[64,128,128]{2,1,0:T(8,128)(2,1)}, bf16[8,8,128,128]{3,2,1,0:T(8,128)(2,1)}, s32[1]{0:T(128)}) custom-call(s32[2]{0:T(128)S(1)} %get-tuple-element.36.start_ref, s32[2]{0:T(128)S(1)} %get-tuple-element.37.turn_ref, bf16[128,128,128]{2,1,0:T(8,128)(2,1)} %bitcast.45, bf16[16,8,128,128]{3,2,1,0:T(8,128)(2,1)} %refs_0_.3), custom_call_target="tpu_custom_call" | custom-call | flops 1000000000 | bytes 4194304 | tf_op jit(solution)/shard_map/pallas_call | solution.py:130
  5.5 3.0 %collective-permute-start.5 = (bf16[8,8,128,128]{3,2,1,0:T(8,128)(2,1)}, bf16[8,8,128,128]{3,2,1,0:T(8,128)(2,1)}, u32[]{:S(2)}, u32[]{:S(2)}) collective-permute-start(bf16[8,8,128,128]{3,2,1,0:T(8,128)(2,1)} %get-tuple-element.12), channel_id=1, source_target_pairs={{0,2},{1,3},{2,0},{3,1},{4,6},{5,7},{6,4},{7,5},{8,10},{9,11},{10,... | collective-permute-start | bytes 6291464 | tf_op jit(solution)/shard_map/ppermute | solution.py:262
  8.5 1.5 %collective-permute-start.2 = (bf16[64,128,128]{2,1,0:T(8,128)(2,1)}, bf16[64,128,128]{2,1,0:T(8,128)(2,1)S(1)}, u32[]{:S(2)}, u32[]{:S(2)}) collective-permute-start(bf16[64,128,128]{2,1,0:T(8,128)(2,1)} %get-tuple-element.10.refs_0_.refs_1_), channel_id=1, source_target_pairs={{0,4},{1,5},{2,30},{3,31},{4,8},{5,9},{6,2},{7,3},{8,12},{9,13},{1... | collective-permute-start | bytes 6291464 | tf_op jit(solution)/shard_map/ppermute | solution.py:262
  10.0 0.1 constant_dynamic-slice_fusion.5
  10.1 0.1 copy.130
  10.2 3.6 %collective-permute-start = (s32[8,8]{1,0:T(8,128)S(1)}, s32[8,8]{1,0:T(8,128)S(1)}, u32[]{:S(2)}, u32[]{:S(2)}) collective-permute-start(s32[8,8]{1,0:T(8,128)S(1)} %copy.130), channel_id=1, source_target_pairs={{0,2},{1,3},{2,0},{3,1},{4,6},{5,7},{6,4},{7,5},{8,10},{9,11},{10,... | collective-permute-start | bytes 776 | tf_op jit(solution)/shard_map/ppermute | solution.py:262
  13.8 0.1 copy.113
  13.9 0.1 copy.114
  13.9 0.1 pad_add_fusion
  14.1 0.1 fusion.6
  14.2 0.2 select_reduce_fusion.3
  14.4 0.6 compare_convert_fusion
  15.0 2.0 %slice.26 = bf16[20,128,128]{2,1,0:T(8,128)(2,1)} slice(bf16[64,128,128]{2,1,0:T(8,128)(2,1)} %get-tuple-element.10.refs_0_.refs_1_), slice={[44:64], [0:128], [0:128]} | slice | bytes 1310720 | tf_op jit(solution)/shard_map/slice | solution.py:289
  16.9 0.1 copy.129
  17.0 37.5 %collective-permute-done = s32[8,8]{1,0:T(8,128)S(1)} collective-permute-done((s32[8,8]{1,0:T(8,128)S(1)}, s32[8,8]{1,0:T(8,128)S(1)}, u32[]{:S(2)}, u32[]{:S(2)}) %collective-permute-start) | collective-permute-done | bytes 288 | tf_op jit(solution)/shard_map/ppermute | solution.py:262
  54.5 4.8 %collective-permute-start.7 = (bf16[20,128,128]{2,1,0:T(8,128)(2,1)}, bf16[20,128,128]{2,1,0:T(8,128)(2,1)}, u32[]{:S(2)}, u32[]{:S(2)}) collective-permute-start(bf16[20,128,128]{2,1,0:T(8,128)(2,1)} %slice.26), channel_id=1, source_target_pairs={{0,28},{1,29},{2,6},{3,7},{4,0},{5,1},{6,10},{7,11},{8,4},{9,5},{1... | collective-permute-start | bytes 1966088 | tf_op jit(solution)/shard_map/ppermute | solution.py:262
  59.3 0.6 fusion.9
  59.9 0.7 reshape.152
  60.6 0.6 reshape.153
  61.3 0.0 copy-start.6
  61.3 1.9 %shard_map.87 = (bf16[12,128,128]{2,1,0:T(8,128)(2,1)}, s32[1]{0:T(128)}) custom-call(s32[1]{0:T(128)} %constant.108.clone.1.start_ref.turn_ref.after_ref, s32[1]{0:T(128)} %constant.108.clone.1.start_ref.turn_ref.after_ref, bf16[64,128,128]{2,1,0:T(8,128)(2,1)S(1)} %collective-permute-done.2.refs_0_.refs_2_.refs_3_), custom_call_target="tpu_custom_call" | custom-call | flops 199999995904 | bytes 4194304 | tf_op jit(solution)/shard_map/pallas_call | solution.py:130
  63.2 0.6 add_add_fusion.2
  63.8 0.6 collective-permute-start.3
  64.4 0.1 copy.123
  64.4 0.1 reshape.160.extra_ref
  64.5 0.1 stack.113.start_ref
  64.6 0.0 collective-permute-start.8
  64.6 0.8 collective-permute-done.3
  65.4 0.1 stack_reshape.3
  65.5 0.1 add.204
  65.6 0.1 copy.116
  65.7 0.1 copy.118
  65.8 0.1 reshape.155
  65.9 0.8 fusion.1
  66.7 0.1 copy.119
  66.8 0.1 iota_compare_fusion
  66.9 0.9 select_reduce_fusion
  67.9 0.1 select_reduce_fusion.1
  68.0 0.1 copy.122
  68.1 0.1 add.212.pick_ref
  68.3 3.6 %shard_map.88.a_ref = bf16[8,32,128,128]{3,2,1,0:T(8,128)(2,1)S(1)} custom-call(s32[1]{0:T(128)} %bitcast.23.first_ref, bf16[16,8,128,128]{3,2,1,0:T(8,128)(2,1)} %refs_0_.3, bf16[16,8,128,128]{3,2,1,0:T(8,128)(2,1)} %collective-permute-done.4.refs_1_, bf16[8,8,128,128]{3,2,1,0:T(8,128)(2,1)} %collective-permute-done.5.refs_2_, ...), custom_call_target="tpu_custom_call" | custom-call | flops 1000000000 | bytes 16777216 | tf_op jit(solution)/shard_map/pallas_call | solution.py:80
  71.9 1.1 collective-permute-done.7.refs_4_
  73.0 2.8 %collective-permute-done.8.refs_5_ = bf16[12,128,128]{2,1,0:T(8,128)(2,1)S(1)} collective-permute-done((bf16[12,128,128]{2,1,0:T(8,128)(2,1)}, bf16[12,128,128]{2,1,0:T(8,128)(2,1)S(1)}, u32[]{:S(2)}, u32[]{:S(2)}) %collective-permute-start.8) | collective-permute-done | bytes 393248 | tf_op jit(solution)/shard_map/ppermute | solution.py:262
  75.9 5.8 %shard_map.89.refs_0_ = bf16[16,128,128]{2,1,0:T(8,128)(2,1)S(1)} custom-call(s32[512]{0:T(512)S(1)} %add.212.pick_ref, s32[6]{0:T(128)S(1)} %stack.113.start_ref, s32[1]{0:T(128)} %constant.108.clone.1.start_ref.turn_ref.after_ref, s32[16]{0:T(128)S(1)} %reshape.160.extra_ref, bf16[8,32,128,128]{3,2,1,0:T(8,128)(2,1)S(1)} %shard_map.88.a_ref, ...), custom_call_target="tpu_custom_call" | custom-call | flops 10737418240 | bytes 25165824 | tf_op jit(solution)/shard_map/pallas_call | solution.py:216
  81.7 2.1 %collective-permute-start.9 = (bf16[16,128,128]{2,1,0:T(8,128)(2,1)S(1)}, bf16[16,128,128]{2,1,0:T(8,128)(2,1)S(1)}, u32[]{:S(2)}, u32[]{:S(2)}) collective-permute-start(bf16[16,128,128]{2,1,0:T(8,128)(2,1)S(1)} %shard_map.89.refs_0_), channel_id=1, source_target_pairs={{0,28},{1,29},{2,6},{3,7},{4,0},{5,1},{6,10},{7,11},{8,4},{9,5},{1... | collective-permute-start | bytes 1572872 | tf_op jit(solution)/shard_map/ppermute | solution.py:262
  83.8 0.1 stack.119.start_ref
  83.9 0.1 fusion.7
  84.0 0.1 pad_add_fusion.3
  84.1 10.7 %collective-permute-done.9.refs_3_ = bf16[16,128,128]{2,1,0:T(8,128)(2,1)S(1)} collective-permute-done((bf16[16,128,128]{2,1,0:T(8,128)(2,1)S(1)}, bf16[16,128,128]{2,1,0:T(8,128)(2,1)S(1)}, u32[]{:S(2)}, u32[]{:S(2)}) %collective-permute-start.9) | collective-permute-done | bytes 524320 | tf_op jit(solution)/shard_map/ppermute | solution.py:262
  94.8 1.8 %collective-permute-done.11.refs_2_.refs_1_ = bf16[16,128,128]{2,1,0:T(8,128)(2,1)S(1)} collective-permute-done((bf16[16,128,128]{2,1,0:T(8,128)(2,1)S(1)}, bf16[16,128,128]{2,1,0:T(8,128)(2,1)S(1)}, u32[]{:S(2)}, u32[]{:S(2)}) %collective-permute-start.11) | collective-permute-done | bytes 524320 | tf_op jit(solution)/shard_map/ppermute | solution.py:262
  96.6 3.2 %collective-permute-start.14 = (bf16[16,128,128]{2,1,0:T(8,128)(2,1)S(1)}, bf16[16,128,128]{2,1,0:T(8,128)(2,1)S(1)}, u32[]{:S(2)}, u32[]{:S(2)}) collective-permute-start(bf16[16,128,128]{2,1,0:T(8,128)(2,1)S(1)} %collective-permute-done.9.refs_3_), channel_id=1, source_target_pairs={{0,2},{1,3},{2,0},{3,1},{4,6},{5,7},{6,4},{7,5},{8,10},{9,11},{10,... | collective-permute-start | bytes 1572872 | tf_op jit(solution)/shard_map/ppermute | solution.py:262
  99.8 0.1 select_reduce_fusion.2
  99.9 0.1 copy.126
  100.1 0.1 add.223.pick_ref
  100.2 2.8 %shard_map.90 = (bf16[2,16,2,32,128]{4,3,2,1,0:T(8,128)(2,1)}, s32[1]{0:T(128)}) custom-call(s32[1]{0:T(128)} %bitcast.column_ref, s32[4]{0:T(128)S(1)} %get-tuple-element.34.slab_ref, s32[4]{0:T(128)S(1)} %get-tuple-element.35.first_ref, bf16[16,128,128]{2,1,0:T(8,128)(2,1)S(1)} %shard_map.89.refs_0_, ...), custom_call_target="tpu_custom_call" | custom-call | flops 1000000000 | bytes 4194304 | tf_op jit(solution)/shard_map/pallas_call | solution.py:173
  103.8 3.5 %shard_map.91.a_ref = bf16[8,32,128,128]{3,2,1,0:T(8,128)(2,1)S(1)} custom-call(s32[1]{0:T(128)} %bitcast.32.first_ref, bf16[16,8,128,128]{3,2,1,0:T(8,128)(2,1)} %refs_0_.3, bf16[16,8,128,128]{3,2,1,0:T(8,128)(2,1)} %collective-permute-done.4.refs_1_, bf16[8,8,128,128]{3,2,1,0:T(8,128)(2,1)} %collective-permute-done.5.refs_2_, ...), custom_call_target="tpu_custom_call" | custom-call | flops 1000000000 | bytes 16777216 | tf_op jit(solution)/shard_map/pallas_call | solution.py:80
  107.3 4.9 %collective-permute-done.14.refs_4_ = bf16[16,128,128]{2,1,0:T(8,128)(2,1)S(1)} collective-permute-done((bf16[16,128,128]{2,1,0:T(8,128)(2,1)S(1)}, bf16[16,128,128]{2,1,0:T(8,128)(2,1)S(1)}, u32[]{:S(2)}, u32[]{:S(2)}) %collective-permute-start.14) | collective-permute-done | bytes 524320 | tf_op jit(solution)/shard_map/ppermute | solution.py:262
  112.1 1.5 %collective-permute-done.13.refs_2_ = bf16[16,128,128]{2,1,0:T(8,128)(2,1)S(1)} collective-permute-done((bf16[16,128,128]{2,1,0:T(8,128)(2,1)S(1)}, bf16[16,128,128]{2,1,0:T(8,128)(2,1)S(1)}, u32[]{:S(2)}, u32[]{:S(2)}) %collective-permute-start.13) | collective-permute-done | bytes 524320 | tf_op jit(solution)/shard_map/ppermute | solution.py:262
  113.7 5.4 %shard_map.92 = f32[8,256]{1,0:T(8,128)S(1)} custom-call(s32[512]{0:T(512)S(1)} %add.223.pick_ref, s32[5]{0:T(128)S(1)} %stack.119.start_ref, s32[1]{0:T(128)} %get-tuple-element.16.after_ref, s32[16]{0:T(128)S(1)} %reshape.160.extra_ref, bf16[8,32,128,128]{3,2,1,0:T(8,128)(2,1)S(1)} %shard_map.91.a_ref, bf16[16,128,128]{2,1,0:T(8,128)(2,1)S(1)} %shard_map.89.refs_0_, ...), custom_call_target="tpu_custom_call" | custom-call | flops 10737418240 | bytes 25165824 | tf_op jit(solution)/shard_map/pallas_call | solution.py:216
  119.0 5.2 %all_gather.3 = f32[4,8,2,128]{3,1,2,0:T(8,128)S(1)} all-gather(f32[1,8,2,128]{3,1,2,0:T(8,128)S(1)} %bitcast.44), channel_id=1, replica_groups=mesh['rows'=8,'blk'=4] {'blk'}, dimensions={0}, use_global_device_ids=true | all-gather | bytes 40960 | tf_op jit(solution)/shard_map/all_gather | solution.py:420
  124.2 0.1 constant_dynamic-slice_fusion
  124.3 0.6 copy.128
  (65 shorter events, 0.2 us)
Async XLA Ops:
  0.6 83.3 %copy-start = (s32[2,16,2]{1,2,0:T(2,128)S(1)}, s32[2,16,2]{1,2,0:T(2,128)}, u32[]{:S(2)}) copy-start(s32[2,16,2]{1,2,0:T(2,128)} %param.13) | copy-start | bytes 772
  0.8 9.3 %copy-start.7 = (s32[16,8]{0,1:T(8,128)S(1)}, s32[16,8]{0,1:T(8,128)}, u32[]{:S(2)}) copy-start(s32[16,8]{0,1:T(8,128)} %param.7) | copy-start | bytes 1540
  0.8 13.0 %copy-start.11 = (s32[2,16,4]{1,2,0:T(4,128)S(1)}, s32[2,16,4]{1,2,0:T(4,128)}, u32[]{:S(2)}) copy-start(s32[2,16,4]{1,2,0:T(4,128)} %param.9) | copy-start | bytes 1540
  0.8 13.1 %copy-start.10 = (s32[2,16,2]{1,2,0:T(2,128)S(1)}, s32[2,16,2]{1,2,0:T(2,128)}, u32[]{:S(2)}) copy-start(s32[2,16,2]{1,2,0:T(2,128)} %param.11) | copy-start | bytes 772
  0.8 13.3 %copy-start.15 = (s32[2,64]{1,0:T(2,128)S(1)}, s32[2,64]{1,0:T(2,128)}, u32[]{:S(2)}) copy-start(s32[2,64]{1,0:T(2,128)} %param.12) | copy-start | bytes 1540
  5.5 55.7 %collective-permute-start.5 = (bf16[8,8,128,128]{3,2,1,0:T(8,128)(2,1)}, bf16[8,8,128,128]{3,2,1,0:T(8,128)(2,1)}, u32[]{:S(2)}, u32[]{:S(2)}) collective-permute-start(bf16[8,8,128,128]{3,2,1,0:T(8,128)(2,1)} %get-tuple-element.12), channel_id=1, source_target_pairs={{0,2},{1,3},{2,0},{3,1},{4,6},{5,7},{6,4},{7,5},{8,10},{9,11},{10,... | collective-permute-start | bytes 6291464 | tf_op jit(solution)/shard_map/ppermute | solution.py:262
  8.5 52.7 %collective-permute-start.2 = (bf16[64,128,128]{2,1,0:T(8,128)(2,1)}, bf16[64,128,128]{2,1,0:T(8,128)(2,1)S(1)}, u32[]{:S(2)}, u32[]{:S(2)}) collective-permute-start(bf16[64,128,128]{2,1,0:T(8,128)(2,1)} %get-tuple-element.10.refs_0_.refs_1_), channel_id=1, source_target_pairs={{0,4},{1,5},{2,30},{3,31},{4,8},{5,9},{6,2},{7,3},{8,12},{9,13},{1... | collective-permute-start | bytes 6291464 | tf_op jit(solution)/shard_map/ppermute | solution.py:262
  10.0 58.2 %collective-permute-start.4 = (bf16[16,8,128,128]{3,2,1,0:T(8,128)(2,1)}, bf16[16,8,128,128]{3,2,1,0:T(8,128)(2,1)}, u32[]{:S(2)}, u32[]{:S(2)}) collective-permute-start(bf16[16,8,128,128]{3,2,1,0:T(8,128)(2,1)} %refs_0_.3), channel_id=1, source_target_pairs={{0,1},{1,0},{2,3},{3,2},{4,5},{5,4},{6,7},{7,6},{8,9},{9,8},{10,11... | collective-permute-start | bytes 12582920 | tf_op jit(solution)/shard_map/ppermute | solution.py:262
  10.2 44.3 %collective-permute-start = (s32[8,8]{1,0:T(8,128)S(1)}, s32[8,8]{1,0:T(8,128)S(1)}, u32[]{:S(2)}, u32[]{:S(2)}) collective-permute-start(s32[8,8]{1,0:T(8,128)S(1)} %copy.130), channel_id=1, source_target_pairs={{0,2},{1,3},{2,0},{3,1},{4,6},{5,7},{6,4},{7,5},{8,10},{9,11},{10,... | collective-permute-start | bytes 776 | tf_op jit(solution)/shard_map/ppermute | solution.py:262
  13.9 49.3 %copy-start.2 = (s32[2,16,4]{2,1,0:T(8,128)}, s32[2,16,4]{2,1,0:T(8,128)S(1)}, u32[]{:S(2)}) copy-start(s32[2,16,4]{2,1,0:T(8,128)S(1)} %copy.113) | copy-start | bytes 1540
  13.9 49.2 %copy-start.3 = (s32[2,16,2]{2,1,0:T(8,128)}, s32[2,16,2]{2,1,0:T(8,128)S(1)}, u32[]{:S(2)}) copy-start(s32[2,16,2]{2,1,0:T(8,128)S(1)} %copy.114) | copy-start | bytes 772
  14.0 46.6 %collective-permute-start.1 = (s32[2,16,6]{2,1,0:T(8,128)S(1)}, s32[2,16,6]{2,1,0:T(8,128)S(1)}, u32[]{:S(2)}, u32[]{:S(2)}) collective-permute-start(s32[2,16,6]{2,1,0:T(8,128)S(1)} %pad_add_fusion), channel_id=1, source_target_pairs={{0,4},{1,29},{2,6},{3,31},{4,8},{5,1},{6,10},{7,3},{8,12},{9,5},{1... | collective-permute-start | bytes 2312 | tf_op jit(solution)/shard_map/ppermute | solution.py:262
  14.2 45.8 %copy-start.8 = (s32[8,2]{0,1:T(2,128)}, s32[8,2]{0,1:T(2,128)S(1)}, u32[]{:S(2)}) copy-start(s32[8,2]{0,1:T(2,128)S(1)} %fusion.6) | copy-start | bytes 196
  54.5 18.5 %collective-permute-start.7 = (bf16[20,128,128]{2,1,0:T(8,128)(2,1)}, bf16[20,128,128]{2,1,0:T(8,128)(2,1)}, u32[]{:S(2)}, u32[]{:S(2)}) collective-permute-start(bf16[20,128,128]{2,1,0:T(8,128)(2,1)} %slice.26), channel_id=1, source_target_pairs={{0,28},{1,29},{2,6},{3,7},{4,0},{5,1},{6,10},{7,11},{8,4},{9,5},{1... | collective-permute-start | bytes 1966088 | tf_op jit(solution)/shard_map/ppermute | solution.py:262
  60.6 0.6 copy-start.5
  61.2 7.0 %collective-permute-start.6 = (bf16[8,8,128,128]{3,2,1,0:T(8,128)(2,1)}, bf16[8,8,128,128]{3,2,1,0:T(8,128)(2,1)}, u32[]{:S(2)}, u32[]{:S(2)}) collective-permute-start(bf16[8,8,128,128]{3,2,1,0:T(8,128)(2,1)} %collective-permute-done.5.refs_2_), channel_id=1, source_target_pairs={{0,1},{1,0},{2,3},{3,2},{4,5},{5,4},{6,7},{7,6},{8,9},{9,8},{10,11... | collective-permute-start | bytes 6291464 | tf_op jit(solution)/shard_map/ppermute | solution.py:262
  61.2 2.0 %copy-start.13 = (s32[192]{0:T(256)S(1)}, s32[192]{0:T(256)}, u32[]{:S(2)}) copy-start(s32[192]{0:T(256)} %reshape.153) | copy-start | bytes 2308
  61.3 2.0 %copy-start.14 = (s32[128]{0:T(128)S(1)}, s32[128]{0:T(128)}, u32[]{:S(2)}) copy-start(s32[128]{0:T(128)} %reshape.152) | copy-start | bytes 1540
  61.3 3.1 %copy-start.12 = (s32[8,2]{0,1:T(2,128)S(1)}, s32[8,2]{0,1:T(2,128)}, u32[]{:S(2)}) copy-start(s32[8,2]{0,1:T(2,128)} %compare_convert_fusion) | copy-start | bytes 196
  61.3 4.2 %copy-start.4 = (s32[8,2,1,8]{3,0,2,1:T(8,128)S(1)}, s32[8,2,1,8]{3,0,2,1:T(8,128)}, u32[]{:S(2)}) copy-start(s32[8,2,1,8]{3,0,2,1:T(8,128)} %get-tuple-element.30) | copy-start | bytes 1540
  61.3 4.6 %copy-start.6 = (s32[2,16,6]{2,1,0:T(8,128)S(1)}, s32[2,16,6]{2,1,0:T(8,128)}, u32[]{:S(2)}) copy-start(s32[2,16,6]{2,1,0:T(8,128)} %copy-done.5) | copy-start | bytes 2308
  61.3 6.6 %copy-start.9 = (s32[8,2]{0,1:T(2,128)S(1)}, s32[8,2]{0,1:T(2,128)}, u32[]{:S(2)}) copy-start(s32[8,2]{0,1:T(2,128)} %copy-done.8) | copy-start | bytes 196
  63.8 1.6 %collective-permute-start.3 = (s32[320]{0:T(512)S(1)}, s32[320]{0:T(512)S(1)}, u32[]{:S(2)}, u32[]{:S(2)}) collective-permute-start(s32[320]{0:T(512)S(1)} %add_add_fusion.2), channel_id=1, source_target_pairs={{0,1},{1,0},{2,3},{3,2},{4,5},{5,4},{6,7},{7,6},{8,9},{9,8},{10,11... | collective-permute-start | bytes 3848 | tf_op jit(solution)/shard_map/ppermute | solution.py:262
  64.6 11.3 %collective-permute-start.8 = (bf16[12,128,128]{2,1,0:T(8,128)(2,1)}, bf16[12,128,128]{2,1,0:T(8,128)(2,1)S(1)}, u32[]{:S(2)}, u32[]{:S(2)}) collective-permute-start(bf16[12,128,128]{2,1,0:T(8,128)(2,1)} %get-tuple-element.13), channel_id=1, source_target_pairs={{0,2},{1,3},{2,0},{3,1},{4,6},{5,7},{6,4},{7,5},{8,10},{9,11},{10,... | collective-permute-start | bytes 1179656 | tf_op jit(solution)/shard_map/ppermute | solution.py:262
  68.3 7.6 %copy-start.1 = (bf16[64,128,128]{2,1,0:T(8,128)(2,1)S(1)}, bf16[64,128,128]{2,1,0:T(8,128)(2,1)}, u32[]{:S(2)}) copy-start(bf16[64,128,128]{2,1,0:T(8,128)(2,1)} %get-tuple-element.10.refs_0_.refs_1_) | copy-start | bytes 6291460
  81.7 13.1 %collective-permute-start.9 = (bf16[16,128,128]{2,1,0:T(8,128)(2,1)S(1)}, bf16[16,128,128]{2,1,0:T(8,128)(2,1)S(1)}, u32[]{:S(2)}, u32[]{:S(2)}) collective-permute-start(bf16[16,128,128]{2,1,0:T(8,128)(2,1)S(1)} %shard_map.89.refs_0_), channel_id=1, source_target_pairs={{0,28},{1,29},{2,6},{3,7},{4,0},{5,1},{6,10},{7,11},{8,4},{9,5},{1... | collective-permute-start | bytes 1572872 | tf_op jit(solution)/shard_map/ppermute | solution.py:262
  83.8 12.8 %collective-permute-start.11 = (bf16[16,128,128]{2,1,0:T(8,128)(2,1)S(1)}, bf16[16,128,128]{2,1,0:T(8,128)(2,1)S(1)}, u32[]{:S(2)}, u32[]{:S(2)}) collective-permute-start(bf16[16,128,128]{2,1,0:T(8,128)(2,1)S(1)} %shard_map.89.refs_0_), channel_id=1, source_target_pairs={{0,2},{1,3},{2,0},{3,1},{4,6},{5,7},{6,4},{7,5},{8,10},{9,11},{10,... | collective-permute-start | bytes 1572872 | tf_op jit(solution)/shard_map/ppermute | solution.py:262
  94.8 5.4 %collective-permute-start.10 = (bf16[16,128,128]{2,1,0:T(8,128)(2,1)S(1)}, bf16[16,128,128]{2,1,0:T(8,128)(2,1)}, u32[]{:S(2)}, u32[]{:S(2)}) collective-permute-start(bf16[16,128,128]{2,1,0:T(8,128)(2,1)S(1)} %shard_map.89.refs_0_), channel_id=1, source_target_pairs={{0,1},{1,0},{2,3},{3,2},{4,5},{5,4},{6,7},{7,6},{8,9},{9,8},{10,11... | collective-permute-start | bytes 1572872 | tf_op jit(solution)/shard_map/ppermute | solution.py:262
  96.6 3.6 %collective-permute-start.12 = (bf16[16,128,128]{2,1,0:T(8,128)(2,1)S(1)}, bf16[16,128,128]{2,1,0:T(8,128)(2,1)}, u32[]{:S(2)}, u32[]{:S(2)}) collective-permute-start(bf16[16,128,128]{2,1,0:T(8,128)(2,1)S(1)} %collective-permute-done.11.refs_2_.refs_1_), channel_id=1, source_target_pairs={{0,1},{1,0},{2,3},{3,2},{4,5},{5,4},{6,7},{7,6},{8,9},{9,8},{10,11... | collective-permute-start | bytes 1572872 | tf_op jit(solution)/shard_map/ppermute | solution.py:262
  96.6 17.0 %collective-permute-start.13 = (bf16[16,128,128]{2,1,0:T(8,128)(2,1)S(1)}, bf16[16,128,128]{2,1,0:T(8,128)(2,1)S(1)}, u32[]{:S(2)}, u32[]{:S(2)}) collective-permute-start(bf16[16,128,128]{2,1,0:T(8,128)(2,1)S(1)} %shard_map.89.refs_0_), channel_id=1, source_target_pairs={{0,4},{1,5},{2,30},{3,31},{4,8},{5,9},{6,2},{7,3},{8,12},{9,13},{1... | collective-permute-start | bytes 1572872 | tf_op jit(solution)/shard_map/ppermute | solution.py:262
  96.6 15.5 %collective-permute-start.14 = (bf16[16,128,128]{2,1,0:T(8,128)(2,1)S(1)}, bf16[16,128,128]{2,1,0:T(8,128)(2,1)S(1)}, u32[]{:S(2)}, u32[]{:S(2)}) collective-permute-start(bf16[16,128,128]{2,1,0:T(8,128)(2,1)S(1)} %collective-permute-done.9.refs_3_), channel_id=1, source_target_pairs={{0,2},{1,3},{2,0},{3,1},{4,6},{5,7},{6,4},{7,5},{8,10},{9,11},{10,... | collective-permute-start | bytes 1572872 | tf_op jit(solution)/shard_map/ppermute | solution.py:262
